TPU v7x, 32 devices: a whole 2x2x4 slice. The times are simulated.
32 devices in a mesh: grp: 4 (over y, x), dev: 8 (over z, core).
Axes of the slice: x: 2, y: 2, z: 4, core: 2. Of those that a mesh axis runs over, the one named last changes fastest.
Arguments:
- cache_k: bfloat16 [64, 8, 256, 128], P('grp', None, 'dev')
- cache_v: bfloat16 [64, 8, 256, 128], P('grp', None, 'dev'), may hold values from -6 to 6
- source: int32 [64], replicated, may hold values from 0 to 63, as said below
- lengths: int32 [64], P('grp'), may hold values from 1 to 255
- query: bfloat16 [64, 6144], P('grp')
- new_key: bfloat16 [64, 8, 128], P('grp'), may hold values from -6 to 6
- new_value: bfloat16 [64, 8, 128], P('grp'), may hold values from -6 to 6
- resid: bfloat16 [64, 6144], P('grp', 'dev'), may hold values from -6 to 6
- out_weight: bfloat16 [6144, 6144], P('dev'), may hold values from -0.078125 to 0.078125
- norm_gain: bfloat16 [6144], replicated, may hold values from 0.099609375 to 1.8984375
- w_gate: bfloat16 [6144, 65536], P(None, ('grp', 'dev')), may hold values from -0.078125 to 0.078125
- w_up: bfloat16 [6144, 65536], P(None, ('grp', 'dev')), may hold values from -0.078125 to 0.078125
- w_down: bfloat16 [65536, 6144], P(('grp', 'dev')), may hold values from -0.0625 to 0.0625
- expert_ids: int32 [64, 2], P('grp'), may hold values from 0 to 7, all different within a row; in each aligned block of 16 rows (0 to 15, 16 to 31, ...) at most 8 rows name the same one
- gate_codes: int32 [64, 2], P('grp'), may hold values from 1 to 1023
Outputs:
- new_cache_k: bfloat16 [64, 8, 256, 128], P('grp', None, 'dev')
- new_cache_v: bfloat16 [64, 8, 256, 128], P('grp', None, 'dev')
- layer_out: bfloat16 [64, 6144], P('grp', 'dev')
Inputs may be any that keep to these rules, and one draw needn't show every extreme that they name: source is a permutation of the 64 slots; each group of 16 slots sends exactly 2 of its requests to each other group and receives exactly 2 from each other group into the slots it vacated; every other slot keeps its own request. `expert_ids`: in the 16 rows of each group no expert is named more than 8 times.
All inputs are finite; a program needn't handle non-finite values.
Results may differ from a plain program's by a relative error of at most 0.012.
Values may be sent and summed in bfloat16 or wider, within the bound.
A program may use at most 128 MiB of HBM per device.

v0:
```python
import jax
import jax.numpy as jnp
from jax import lax
from jax.sharding import PartitionSpec as P

EXPERTS = 8
TOP = 2
MOVE = 2
CAP = 8


def joined(array, axis, combine):
    everything = jax.tree.map(
        lambda part, kind: lax.all_gather(part.astype(kind), axis),
        array,
        (jnp.bfloat16, jnp.bfloat16, jnp.bfloat16),
    )

    def take(k):
        return jax.tree.map(lambda part, own: part[k].astype(own.dtype), everything, array)

    return lax.fori_loop(
        1, lax.axis_size(axis), lambda k, so_far: combine(so_far, take(k)), take(0)
    )


def expert_ffn(rows, w_gate, w_up, w_down):
    gate_val = jnp.dot(rows, w_gate, preferred_element_type=jnp.float32)
    up_val = jnp.dot(rows, w_up, preferred_element_type=jnp.float32)
    hidden = (jax.nn.silu(gate_val) * up_val).astype(jnp.bfloat16)
    return jnp.dot(hidden, w_down, preferred_element_type=jnp.float32)


def merge_states(earlier, later):
    top = jnp.maximum(earlier[0], later[0])
    first_scale = jnp.exp(earlier[0] - top)
    second_scale = jnp.exp(later[0] - top)
    totals = earlier[1] * first_scale + later[1] * second_scale
    context = earlier[2] * first_scale[..., None] + later[2] * second_scale[..., None]
    return (top, totals, context)


def on_device(
    cache_k,
    cache_v,
    source,
    lengths,
    query,
    new_key,
    new_value,
    resid,
    out_weight,
    norm_gain,
    w_gate,
    w_up,
    w_down,
    expert_ids,
    gate_codes,
):
    group_count = lax.axis_size("grp")
    dev_count = lax.axis_size("dev")
    group_id = lax.axis_index("grp")
    dev_id = lax.axis_index("dev")
    per_group, kv_heads, block_len, head_dim = cache_k.shape
    all_slots = source.shape[0]
    model_width = resid.shape[1] * dev_count
    feat_width = resid.shape[1]
    slot_range = jnp.arange(all_slots, dtype=jnp.int32)
    inverse = jnp.sum(
        jnp.where(source[:, None] == slot_range[None, :], slot_range[:, None], 0), axis=0
    )
    old_group = slot_range // per_group
    dest_group = inverse // per_group
    leaving = dest_group != old_group
    same_route = (old_group[:, None] == old_group[None, :]) & (
        dest_group[:, None] == dest_group[None, :]
    )
    earlier_movers = same_route & leaving[None, :] & (slot_range[None, :] < slot_range[:, None])
    mover_rank = jnp.sum(earlier_movers.astype(jnp.int32), axis=1)
    first_slot = group_id * per_group
    my_leaving = lax.dynamic_slice_in_dim(leaving, first_slot, per_group)
    my_dest = lax.dynamic_slice_in_dim(dest_group, first_slot, per_group)
    my_rank = lax.dynamic_slice_in_dim(mover_rank, first_slot, per_group)
    buffer_range = jnp.arange(group_count * MOVE, dtype=jnp.int32)
    local_range = jnp.arange(per_group, dtype=jnp.int32)
    match = (
        my_leaving[None, :]
        & (my_dest[None, :] == (buffer_range // MOVE)[:, None])
        & (my_rank[None, :] == (buffer_range % MOVE)[:, None])
    )
    picked = jnp.sum(jnp.where(match, local_range[None, :], 0), axis=1)
    filled = jnp.any(match, axis=1)[:, None, None, None]
    zero_block = jnp.zeros((), jnp.bfloat16)
    send_k = jnp.where(filled, jnp.take(cache_k, picked, axis=0), zero_block)
    send_v = jnp.where(filled, jnp.take(cache_v, picked, axis=0), zero_block)
    recv_k, recv_v = (
        lax.all_to_all(send_k, "grp", split_axis=0, concat_axis=0, tiled=True),
        lax.all_to_all(send_v, "grp", split_axis=0, concat_axis=0, tiled=True),
    )
    my_source = lax.dynamic_slice_in_dim(source, first_slot, per_group)
    source_group = my_source // per_group
    arrival = per_group + source_group * MOVE + jnp.take(mover_rank, my_source)
    where_from = jnp.where(source_group == group_id, my_source - first_slot, arrival)
    moved_k = jnp.take(jnp.concatenate([cache_k, recv_k], axis=0), where_from, axis=0)
    moved_v = jnp.take(jnp.concatenate([cache_v, recv_v], axis=0), where_from, axis=0)
    positions = dev_id * block_len + jnp.arange(block_len, dtype=jnp.int32)
    hit = (positions[None, :] == lengths[:, None])[:, None, :, None]
    new_cache_k = jnp.where(hit, new_key[:, :, None, :], moved_k)
    new_cache_v = jnp.where(hit, new_value[:, :, None, :], moved_v)
    share_heads = query.shape[1] // (kv_heads * head_dim)
    grouped = query.reshape(per_group, kv_heads, share_heads, head_dim)
    scores = (
        jnp.einsum("rkgh,rkph->rkgp", grouped, new_cache_k, preferred_element_type=jnp.float32)
        / head_dim**0.5
    )
    valid = (positions[None, :] <= lengths[:, None])[:, None, None, :]
    scores = jnp.where(valid, scores, jnp.float32(-1e30))
    local_peak = jnp.max(scores, axis=-1)
    values_wide = new_cache_v.astype(jnp.float32)
    weights = jnp.where(valid, jnp.exp(scores - local_peak[..., None]), jnp.float32(0.0))
    local_total = jnp.sum(weights, axis=-1)
    local_context = jnp.einsum(
        "rkgp,rkph->rkgh", weights, values_wide, precision=lax.Precision.HIGHEST
    )
    peak, totals, context = joined((local_peak, local_total, local_context), "dev", merge_states)
    attn = (context / totals[..., None]).reshape(per_group, -1).astype(jnp.bfloat16)
    row_count = out_weight.shape[0]
    attn_mine = lax.dynamic_slice_in_dim(attn, dev_id * row_count, row_count, 1)
    partial_value = jnp.dot(attn_mine, out_weight, preferred_element_type=jnp.float32)
    expert_range = jnp.arange(EXPERTS, dtype=jnp.int32)
    onehot = expert_ids[:, :, None] == expert_range[None, None, :]
    flat_hot = onehot.reshape(per_group * TOP, EXPERTS).astype(jnp.int32)
    before = jnp.cumsum(flat_hot, axis=0) - flat_hot
    route_rank = jnp.sum(before * flat_hot, axis=1).reshape(per_group, TOP)
    slot_hot = (route_rank[:, :, None] == jnp.arange(CAP, dtype=jnp.int32)[None, None, :]).astype(
        jnp.float32
    )
    codes = gate_codes.astype(jnp.float32)
    gate_weight = codes / jnp.sum(codes, axis=-1, keepdims=True)
    selector = jnp.einsum("tke,tkc->ect", onehot.astype(jnp.float32), slot_hot)
    weighted_sel = jnp.einsum("tke,tkc,tk->ect", onehot.astype(jnp.float32), slot_hot, gate_weight)
    col_start = dev_id * feat_width
    split = group_count * dev_count // EXPERTS
    share = lax.psum_scatter(
        partial_value.astype(jnp.bfloat16), "dev", scatter_dimension=1, tiled=True
    ).astype(jnp.float32)
    mixed = resid.astype(jnp.float32) + share
    total_sq = lax.psum(jnp.sum(mixed * mixed, axis=1), "dev")
    gain_mine = lax.dynamic_slice_in_dim(norm_gain, col_start, feat_width).astype(jnp.float32)
    normed = (
        mixed * lax.rsqrt(total_sq / model_width + 1e-05)[:, None] * gain_mine[None, :]
    ).astype(jnp.bfloat16)
    slot_rows = jnp.einsum(
        "ect,tf->ecf", selector.astype(jnp.bfloat16), normed, preferred_element_type=jnp.float32
    ).astype(jnp.bfloat16)
    send_rows = jnp.broadcast_to(slot_rows[:, None], (EXPERTS, split, CAP, feat_width)).reshape(
        group_count * dev_count, CAP, feat_width
    )
    received = lax.all_to_all(send_rows, ("grp", "dev"), split_axis=0, concat_axis=0, tiled=True)
    slot_count = received.shape[1]
    rows = (
        received.reshape(group_count, dev_count, slot_count, feat_width)
        .transpose(0, 2, 1, 3)
        .reshape(group_count * slot_count, model_width)
    )
    outputs = expert_ffn(rows, w_gate, w_up, w_down)
    back = (
        outputs.reshape(group_count, slot_count, dev_count, feat_width)
        .transpose(0, 2, 1, 3)
        .reshape(group_count * dev_count, slot_count, feat_width)
    )
    returned = lax.all_to_all(
        back.astype(jnp.bfloat16), ("grp", "dev"), split_axis=0, concat_axis=0, tiled=True
    ).astype(back.dtype)
    expert_sums = jnp.sum(returned.reshape(EXPERTS, split, CAP, feat_width), axis=1)
    moe = jnp.einsum("ect,ecf->tf", weighted_sel, expert_sums, precision=lax.Precision.HIGHEST)
    layer_out = (mixed + moe).astype(jnp.bfloat16)
    return (new_cache_k, new_cache_v, layer_out)


def solution(mesh):
    in_specs = (
        P("grp", None, "dev", None),
        P("grp", None, "dev", None),
        P(),
        P("grp"),
        P("grp", None),
        P("grp", None, None),
        P("grp", None, None),
        P("grp", "dev"),
        P("dev", None),
        P(),
        P(None, ("grp", "dev")),
        P(None, ("grp", "dev")),
        P(("grp", "dev"), None),
        P("grp", None),
        P("grp", None),
    )
    out_specs = (P("grp", None, "dev", None), P("grp", None, "dev", None), P("grp", "dev"))
    return jax.shard_map(
        on_device, mesh=mesh, in_specs=in_specs, out_specs=out_specs, check_vma=False
    )
```

profile of v0, /device:TPU:0, one launch (start us, length us, event | category | flops | bytes accessed | tf_op | source)
XLA Modules:
  0.0 214.9 jit_solution(9731184885976008298)
XLA Ops:
  8.8 1.9 gather_fusion.1
  10.7 1.9 gather_fusion.3
  12.6 1.2 select_select_fusion.2
  13.7 5.2 %all-to-all-start = ((bf16[8,8,32,128]{3,2,1,0:T(8,128)(2,1)}), bf16[8,8,32,128]{3,2,1,0:T(8,128)(2,1)S(1)}, u32[]{:S(2)}, u32[]{:S(2)}) async-start(bf16[8,8,32,128]{3,2,1,0:T(8,128)(2,1)} %get-tuple-element.232), calls=%async_computation | async-start | bytes 1048576 | tf_op jit(solution)/shard_map/all_to_all | solution.py:97
  21.0 5.9 %all-to-all-done = bf16[8,8,32,128]{3,2,1,0:T(8,128)(2,1)S(1)} async-done(((bf16[8,8,32,128]{3,2,1,0:T(8,128)(2,1)}), bf16[8,8,32,128]{3,2,1,0:T(8,128)(2,1)S(1)}, u32[]{:S(2)}, u32[]{:S(2)}) %all-to-all-start) | async-done | bytes 524320 | tf_op jit(solution)/shard_map/all_to_all | solution.py:97
  26.9 3.5 %all-to-all-start.1 = ((bf16[8,8,32,128]{3,2,1,0:T(8,128)(2,1)}), bf16[8,8,32,128]{3,2,1,0:T(8,128)(2,1)S(1)}, u32[]{:S(2)}, u32[]{:S(2)}) async-start(bf16[8,8,32,128]{3,2,1,0:T(8,128)(2,1)} %get-tuple-element.231), calls=%async_computation.1 | async-start | bytes 1048576 | tf_op jit(solution)/shard_map/all_to_all | solution.py:98
  30.4 1.2 reshape.231
  32.4 1.4 pad_maximum_fusion
  34.5 3.0 %all-to-all-done.1 = bf16[8,8,32,128]{3,2,1,0:T(8,128)(2,1)S(1)} async-done(((bf16[8,8,32,128]{3,2,1,0:T(8,128)(2,1)}), bf16[8,8,32,128]{3,2,1,0:T(8,128)(2,1)S(1)}, u32[]{:S(2)}, u32[]{:S(2)}) %all-to-all-start.1) | async-done | bytes 524320 | tf_op jit(solution)/shard_map/all_to_all | solution.py:98
  37.5 1.4 pad_maximum_fusion.1
  38.9 1.7 gather_fusion.4
  40.5 1.5 select_select_fusion
  43.7 1.0 convolution_convert_fusion.2
  46.3 14.9 %all-gather.1 = bf16[128,8,6]{2,1,0:T(8,128)(2,1)S(1)} all-gather(bf16[16,8,6]{2,1,0:T(8,128)(2,1)S(1)} %fusion.9), channel_id=3, replica_groups=mesh['grp'=4,'dev'=8] {'dev'}, dimensions={0}, use_global_device_ids=true | all-gather | bytes 13824 | tf_op jit(solution)/shard_map/all_gather | solution.py:14
  61.9 15.1 %all-gather = bf16[128,8,6]{2,1,0:T(8,128)(2,1)S(1)} all-gather(bf16[16,8,6]{2,1,0:T(8,128)(2,1)S(1)} %convert_element_type.150), channel_id=2, replica_groups=mesh['grp'=4,'dev'=8] {'dev'}, dimensions={0}, use_global_device_ids=true | all-gather | bytes 13824 | tf_op jit(solution)/shard_map/all_gather | solution.py:14
  78.7 12.4 %while.19 = (s32[]{:T(128)}, f32[16,8,6]{0,1,2:T(8,128)S(1)}, f32[16,8,6]{0,1,2:T(8,128)S(1)}, f32[16,8,6,128]{3,2,1,0:T(8,128)S(1)}, bf16[8,16,8,6]{1,2,3,0:T(8...) while((s32[]{:T(128)}, f32[16,8,6]{0,1,2:T(8,128)S(1)}, ...), condition=%wide.region_7.10_spmd, body=%wide.region_6.9_spmd.sunk | while | flops 399365 | bytes 1416343 | solution.py:22
  91.7 5.7 %convolution_convert_fusion.1 = bf16[16,6144]{1,0:T(8,128)(2,1)} fusion(bf16[768,6144]{1,0:T(8,128)(2,1)} %param.29, bf16[16,6144]{1,0:T(8,128)(2,1)S(1)} %convert_element_type.162, s32[]{:T(128)S(6)} %select_n.152), kind=kOutput, calls=%fused_computation.16 | convolution fusion | flops 151093248 | bytes 9658372 | tf_op jit(solution)/shard_map/dot_general | solution.py:129
  98.9 29.1 %reduce-scatter.2.cloned.1.call-done = bf16[16,768]{1,0:T(8,128)(2,1)} async-done(((bf16[16,6144]{1,0:T(8,128)(2,1)}), bf16[16,768]{1,0:T(8,128)(2,1)}) %reduce-scatter.2.cloned.1.call-update) | async-done | bytes 24592 | tf_op jit(solution)/shard_map/reduce_scatter | solution.py:144
  128.9 13.7 %psum.7 = f32[16]{0:T(128)S(1)} all-reduce(f32[16]{0:T(128)S(1)} %multiply_reduce_fusion), channel_id=1, replica_groups=mesh['grp'=4,'dev'=8] {'dev'}, use_global_device_ids=true, to_apply=%region_13.16 | all-reduce | flops 16 | bytes 128 | tf_op jit(solution)/shard_map/psum | solution.py:148
  143.6 16.3 %all_to_all.20 = bf16[32,8,768]{2,1,0:T(8,128)(2,1)S(1)} all-to-all(bf16[32,8,768]{2,1,0:T(8,128)(2,1)S(1)} %bitcast.64), channel_id=1, replica_groups=mesh['grp'=4,'dev'=8] {'grp','dev'}, dimensions={0} | all-to-all | bytes 786432 | tf_op jit(solution)/shard_map/all_to_all | solution.py:159
  159.9 10.4 %fusion.42 = f32[32,2048]{1,0:T(8,128)S(1)} fusion(bf16[32,6144]{1,0:T(8,128)(2,1)S(1)} %bitcast.62, bf16[6144,2048]{1,0:T(8,128)(2,1)} %param.31), kind=kOutput, calls=%fused_computation.120 | convolution fusion | flops 805306368 | bytes 25821184 | tf_op jit(solution)/shard_map/dot_general | solution.py:28
  170.4 20.6 %convolution_convert_fusion = bf16[32,6144]{1,0:T(8,128)(2,1)} fusion(bf16[2048,6144]{1,0:T(8,128)(2,1)} %param.33, bf16[32,6144]{1,0:T(8,128)(2,1)S(1)} %bitcast.63, bf16[6144,2048]{1,0:T(8,128)(2,1)} %param.32, f32[32,2048]{1,0:T(8,128)S(1)} %fusion.42), kind=kOutput, calls=%fused_computation.15 | convolution fusion | flops 1611202560 | bytes 51380224 | tf_op jit(solution)/shard_map/dot_general | solution.py:31
  190.9 2.6 %all-to-all-start.3 = ((bf16[32,8,768]{2,1,0:T(8,128)(2,1)}), bf16[32,8,768]{2,1,0:T(8,128)(2,1)S(1)}, u32[]{:S(2)}, u32[]{:S(2)}) async-start(bf16[32,8,768]{2,1,0:T(8,128)(2,1)} %bitcast.19), calls=%async_computation.4 | async-start | bytes 786432 | tf_op jit(solution)/shard_map/all_to_all | solution.py:172
  194.2 12.9 %all-to-all-done.3 = bf16[32,8,768]{2,1,0:T(8,128)(2,1)S(1)} async-done(((bf16[32,8,768]{2,1,0:T(8,128)(2,1)}), bf16[32,8,768]{2,1,0:T(8,128)(2,1)S(1)}, u32[]{:S(2)}, u32[]{:S(2)}) %all-to-all-start.3) | async-done | bytes 393248 | tf_op jit(solution)/shard_map/all_to_all | solution.py:172
  (112 shorter events, 28.4 us)
Async XLA Ops:
  7.2 33.3 %copy-start.5 = (bf16[16,8,128]{2,1,0:T(8,128)(2,1)S(1)}, bf16[16,8,128]{2,1,0:T(8,128)(2,1)}, u32[]{:S(2)}) copy-start(bf16[16,8,128]{2,1,0:T(8,128)(2,1)} %param.26) | copy-start | bytes 98308
  7.2 33.3 %copy-start.4 = (bf16[16,8,128]{2,1,0:T(8,128)(2,1)S(1)}, bf16[16,8,128]{2,1,0:T(8,128)(2,1)}, u32[]{:S(2)}) copy-start(bf16[16,8,128]{2,1,0:T(8,128)(2,1)} %param.27) | copy-start | bytes 98308
  13.7 13.2 %all-to-all-start = ((bf16[8,8,32,128]{3,2,1,0:T(8,128)(2,1)}), bf16[8,8,32,128]{3,2,1,0:T(8,128)(2,1)S(1)}, u32[]{:S(2)}, u32[]{:S(2)}) async-start(bf16[8,8,32,128]{3,2,1,0:T(8,128)(2,1)} %get-tuple-element.232), calls=%async_computation | async-start | bytes 1048576 | tf_op jit(solution)/shard_map/all_to_all | solution.py:97
  26.9 10.6 %all-to-all-start.1 = ((bf16[8,8,32,128]{3,2,1,0:T(8,128)(2,1)}), bf16[8,8,32,128]{3,2,1,0:T(8,128)(2,1)S(1)}, u32[]{:S(2)}, u32[]{:S(2)}) async-start(bf16[8,8,32,128]{3,2,1,0:T(8,128)(2,1)} %get-tuple-element.231), calls=%async_computation.1 | async-start | bytes 1048576 | tf_op jit(solution)/shard_map/all_to_all | solution.py:98
  30.4 47.3 %all-gather.5.cloned.1.call-start = ((), (), s32[]{:S(2)}) async-start(), calls=%async_computation.6 | async-start | bytes 1769472 | tf_op jit(solution)/shard_map/all_gather | solution.py:14
  32.4 13.2 %copy-start.6 = (s32[16,2]{0,1:T(2,128)S(1)}, s32[16,2]{0,1:T(2,128)}, u32[]{:S(2)}) copy-start(s32[16,2]{0,1:T(2,128)} %param.34) | copy-start | bytes 388
  42.0 1.0 copy-start.1
  42.1 36.7 %copy-start = (bf16[16,8,32,128]{3,2,1,0:T(8,128)(2,1)}, bf16[16,8,32,128]{3,2,1,0:T(8,128)(2,1)S(1)}, u32[]{:S(2)}) copy-start(bf16[16,8,32,128]{3,2,1,0:T(8,128)(2,1)S(1)} %get-tuple-element.227) | copy-start | bytes 3145732
  45.5 82.6 %reduce-scatter.2.cloned.1.call-start = ((), (), s32[]{:S(2)}) async-start(), calls=%async_computation.5 | async-start | bytes 221184 | tf_op jit(solution)/shard_map/reduce_scatter | solution.py:144
  91.1 36.9 %copy-start.2 = (bf16[16,768]{1,0:T(8,128)(2,1)S(1)}, bf16[16,768]{1,0:T(8,128)(2,1)}, u32[]{:S(2)}) copy-start(bf16[16,768]{1,0:T(8,128)(2,1)} %param.28) | copy-start | bytes 73732
  170.3 23.2 %copy-start.7 = (s32[16,2]{0,1:T(2,128)S(1)}, s32[16,2]{0,1:T(2,128)}, u32[]{:S(2)}) copy-start(s32[16,2]{0,1:T(2,128)} %param.35) | copy-start | bytes 388
  170.4 36.8 %copy-start.3 = (bf16[16,768]{1,0:T(8,128)(2,1)S(1)}, bf16[16,768]{1,0:T(8,128)(2,1)}, u32[]{:S(2)}) copy-start(bf16[16,768]{1,0:T(8,128)(2,1)} %reduce-scatter.2.cloned.1.call-done) | copy-start | bytes 73732
  190.9 16.1 %all-to-all-start.3 = ((bf16[32,8,768]{2,1,0:T(8,128)(2,1)}), bf16[32,8,768]{2,1,0:T(8,128)(2,1)S(1)}, u32[]{:S(2)}, u32[]{:S(2)}) async-start(bf16[32,8,768]{2,1,0:T(8,128)(2,1)} %bitcast.19), calls=%async_computation.4 | async-start | bytes 786432 | tf_op jit(solution)/shard_map/all_to_all | solution.py:172
Sparse Core Ops, SparseCore 0:
  45.6 27.4 all-gather.4
  97.6 30.4 reduce-scatter.1
where the time goes:
time: 216 us; the launch traced here: 215 us
  blocking collectives  60 us (28%)
  waiting for transfers between devices  50.9 us (24%)
  matrix products  40.9 us (19%)
  local copies, waits for them, and re-layouts  20.7 us (10%)
  other arithmetic  16.3 us (8%)
  between operations  14.3 us (7%)
  starting transfers between devices  11.3 us (5%)
    all_gather x2, blocking collectives, joined(): lax.all_gather(part.astype(kind), axis)  30 us
    reduce_scatter x1, waiting for transfers between devices, on_device(): lax.psum_scatter(partial_value.astype(jnp.bfloat16), 'dev', scatter_dimen...  29.1 us
    dot_general x1, matrix products, expert_ffn(): return jnp.dot(hidden, w_down, preferred_element_type=jnp.float32)  20.6 us
    all_to_all x1, blocking collectives, on_device(): lax.all_to_all(send_rows, ('grp', 'dev'), split_axis=0, concat_axis=0, ti...  16.3 us
    psum x1, blocking collectives, on_device(): total_sq = lax.psum(jnp.sum(mixed * mixed, axis=1), 'dev')  13.7 us
    all_to_all x1, waiting for transfers between devices, on_device(): lax.all_to_all(back.astype(jnp.bfloat16), ('grp', 'dev'), split_axis=0, c...  12.9 us
    dot_general x1, matrix products, expert_ffn(): gate_val = jnp.dot(rows, w_gate, preferred_element_type=jnp.float32)  10.4 us
    dynamic_slice x7, local copies, waits for them, and re-layouts, take(): part[k].astype(own.dtype)  6.59 us
  transfers between devices with their start and end apart: 5, of which 4 were waited for; matrix products, arithmetic and copies ran while one was open for 5% of the time, Pallas kernels for 0%

commit v1 on v0

--- a/solution.py
+++ b/solution.py
@@ -1,6 +1,8 @@
 import jax
 import jax.numpy as jnp
 from jax import lax
+from jax.experimental import pallas as pl
+from jax.experimental.pallas import tpu as pltpu
 from jax.sharding import PartitionSpec as P
 
 EXPERTS = 8
@@ -178,6 +180,489 @@
     return (new_cache_k, new_cache_v, layer_out)
 
 
+MESH = pl.DeviceIdType.MESH
+BF = jnp.bfloat16
+F32 = jnp.float32
+SLOTS = 17
+NT = 512
+
+
+def ask(cond):
+    return cond.astype(jnp.int32)
+
+
+def layer_kernel(
+    ck_hbm, cv_hbm, source, lengths, query, new_key, new_value, resid, ow_hbm, gain,
+    wg_hbm, wu_hbm, wd_hbm, ids_ref, codes_ref,
+    nk_hbm, nv_hbm, out_ref,
+    ck, cv, rk, rv, sk, sv, nk, nv,
+    mask_ref, cs, cr, ss, sr, attn_ref, po, pr, mixed_ref,
+    d1s, d1r, d2s, xr, acc_g, acc_u, hid, oacc, r1s, r1r, r2s, r2r, r3s, r3r, wt_ref,
+    wbuf, wsem, csem, osem,
+    ms_send, ms_recv, a_send, a_recv, st_send, st_recv, p_send, p_recv,
+    e1_send, e1_recv, e2_send, e2_recv, e3_send, e3_recv,
+    b1_send, b1_recv, b2_send, b2_recv, b3_send, b3_recv,
+):
+    G, N = 4, 8
+    g = lax.axis_index("grp")
+    d = lax.axis_index("dev")
+    z, c = d // 2, d % 2
+    feat = resid.shape[1]
+    width = feat * N
+    hidden = wbuf.shape[2]
+    block_len = ck.shape[2]
+
+    def grp_peer(i):
+        return (lax.rem(g + i, G), d)
+
+    def dev_peer(i):
+        return (g, lax.rem(d + i, N))
+
+    def z_peer(i):
+        return (g, lax.rem(z + i, 4) * 2 + c)
+
+    sibling = (g, z * 2 + 1 - c)
+
+    def chunk_dev(k):
+        return lax.rem(z + k % 4, 4) * 2 + (c if k < 4 else 1 - c)
+
+    def remote(src, dst, send, recv, to):
+        return pltpu.make_async_remote_copy(
+            src_ref=src, dst_ref=dst, send_sem=send, recv_sem=recv, device_id=to, device_id_type=MESH
+        )
+
+    own_k = pltpu.make_async_copy(ck_hbm, ck, csem.at[0])
+    own_v = pltpu.make_async_copy(cv_hbm, cv, csem.at[1])
+    own_k.start()
+    own_v.start()
+
+    def load_rows(hbm, rows, slot, sem):
+        return pltpu.make_async_copy(
+            hbm.at[pl.ds(pl.multiple_of(rows, feat), feat)], wbuf.at[slot], wsem.at[sem]
+        )
+
+    out_loads = [
+        pltpu.make_async_copy(ow_hbm.at[:, pl.ds(b * hidden, hidden)], wbuf.at[b], wsem.at[b])
+        for b in range(3)
+    ]
+    gate_loads = [load_rows(wg_hbm, chunk_dev(k) * feat, 3 + k, 3 + k) for k in range(8)]
+    up_slot = [11, 12, 13, 14, 15, 16, 0, 1]
+    up_loads = [load_rows(wu_hbm, chunk_dev(k) * feat, up_slot[k], 11 + k) for k in range(8)]
+    down_slot = [2, 3, 11, 4, 12, 5, 13, 6, 14]
+    down_rows = [(0, feat), (feat, feat), (2 * feat, hidden - 2 * feat)]
+    down_loads = []
+    for n in range(9):
+        col, (start, size) = n // 3, down_rows[n % 3]
+        down_loads.append(
+            pltpu.make_async_copy(
+                wd_hbm.at[pl.ds(start, size), pl.ds(col * hidden, hidden)],
+                wbuf.at[down_slot[n], pl.ds(0, size)],
+                wsem.at[19 + n],
+            )
+        )
+
+    barrier = pltpu.get_barrier_semaphore()
+    for i in range(1, G):
+        pl.semaphore_signal(barrier, inc=1, device_id=grp_peer(i), device_id_type=MESH)
+    for i in range(1, N):
+        pl.semaphore_signal(barrier, inc=1, device_id=dev_peer(i), device_id_type=MESH)
+    for load in out_loads:
+        load.start()
+    for k in range(8):
+        gate_loads[k].start()
+        if k < 6:
+            up_loads[k].start()
+
+    zero = jnp.int32(0)
+    own_k.wait()
+    own_v.wait()
+    for i in range(1, G):
+        q = lax.rem(g + i, G)
+        first, second, seen = zero, zero, zero
+        for s in range(16):
+            v = source[q * 16 + s] - g * 16
+            mine = ask(v >= 0) * ask(v < 16)
+            first = first + mine * ask(seen == 0) * v
+            second = second + mine * ask(seen == 1) * v
+            seen = seen + mine
+        at = 2 * (i - 1)
+        sk[at] = ck[first]
+        sk[at + 1] = ck[second]
+        sv[at] = cv[first]
+        sv[at + 1] = cv[second]
+
+    pl.semaphore_wait(barrier, G - 1 + N - 1)
+
+    moves = []
+    for i in range(1, G):
+        part = pl.ds(2 * (i - 1), 2)
+        for t, (src, dst) in enumerate(((sk, rk), (sv, rv))):
+            move = remote(
+                src.at[part], dst.at[part], ms_send.at[t, i], ms_recv.at[t, i], grp_peer(i)
+            )
+            move.start()
+            moves.append(move)
+
+    lane = lax.broadcasted_iota(jnp.int32, (96, 16 * block_len), 1)
+    row = lax.broadcasted_iota(jnp.int32, (96, 16 * block_len), 0)
+    limit = jnp.zeros((96, 16 * block_len), jnp.int32)
+    for s in range(16):
+        limit = jnp.where(lane // block_len == s, lengths[s], limit)
+    inside = (d * block_len + lane % block_len <= limit) & (lane // block_len == row % 16)
+    mask_ref[...] = jnp.where(inside, 1.0, 0.0)
+
+    expert_of = lax.broadcasted_iota(jnp.int32, (16, 64), 1) // 8
+    slot_of = lax.broadcasted_iota(jnp.int32, (16, 64), 1) % 8
+    codes = codes_ref[...].astype(F32)
+    total_code = codes[:, 0:1] + codes[:, 1:2]
+    hot0 = jnp.where(ids_ref[:, 0:1] == expert_of, 1.0, 0.0)
+    hot1 = jnp.where(ids_ref[:, 1:2] == expert_of, 1.0, 0.0)
+    hot = hot0 + hot1
+    t_row = lax.broadcasted_iota(jnp.int32, (16, 16), 0)
+    t_col = lax.broadcasted_iota(jnp.int32, (16, 16), 1)
+    lower = jnp.where(t_col < t_row, 1.0, 0.0).astype(BF)
+    rank = jnp.dot(lower, hot.astype(BF), preferred_element_type=F32)
+    placed = jnp.where(rank == slot_of.astype(F32), 1.0, 0.0)
+    wt_ref[0] = hot * placed
+    wt_ref[1] = (hot0 * (codes[:, 0:1] / total_code) + hot1 * (codes[:, 1:2] / total_code)) * placed
+
+    for move in moves:
+        move.wait_recv()
+
+    counts = [zero] * G
+    p_iota = lax.broadcasted_iota(jnp.int32, (8, block_len, 128), 1)
+    for s in range(16):
+        origin = source[g * 16 + s] // 16
+        off = lax.rem(g - origin + G, G)
+        at = zero
+        for i in range(1, G):
+            here = ask(off == i)
+            at = at + here * (2 * (i - 1) + counts[i])
+            counts[i] = counts[i] + here
+        at = jnp.minimum(at, 5)
+        stays = jnp.full((8, block_len, 128), off, jnp.int32) == 0
+        hit = p_iota == lengths[s] - d * block_len
+        for own, got, new, dst in ((ck, rk, new_key, nk), (cv, rv, new_value, nv)):
+            kept = jnp.where(stays, own[s].astype(F32), got[at].astype(F32))
+            fresh = jnp.broadcast_to(new[s].astype(F32)[:, None, :], (8, block_len, 128))
+            dst[s] = jnp.where(hit, fresh, kept).astype(BF)
+
+    put_k = pltpu.make_async_copy(nk, nk_hbm, osem.at[0])
+    put_v = pltpu.make_async_copy(nv, nv_hbm, osem.at[1])
+    put_k.start()
+    put_v.start()
+
+    stat_lane = lax.broadcasted_iota(jnp.int32, (96, 128), 1)
+
+    def attend(i):
+        h = lax.rem(d + i, N)
+        rows = [
+            query[:, pl.ds(pl.multiple_of((h * 6 + j) * 128, 128), 128)] for j in range(6)
+        ]
+        q_h = jnp.concatenate(rows, axis=0)
+        k_h = nk[:, pl.ds(h, 1)].reshape(16 * block_len, 128)
+        v_h = nv[:, pl.ds(h, 1)].reshape(16 * block_len, 128)
+        valid = mask_ref[...] > 0.5
+        scores = lax.dot_general(q_h, k_h, (((1,), (1,)), ((), ())), preferred_element_type=F32)
+        scores = jnp.where(valid, scores / 128**0.5, F32(-1e30))
+        peak = jnp.max(scores, axis=1, keepdims=True)
+        weights = jnp.where(valid, jnp.exp(scores - peak), 0.0)
+        total = jnp.sum(weights, axis=1, keepdims=True)
+        cs[i] = jnp.dot(weights.astype(BF), v_h, preferred_element_type=F32).astype(BF)
+        stat = jnp.where(stat_lane == 0, peak, jnp.where(stat_lane == 1, total, 0.0))
+        stat = jnp.concatenate([stat, jnp.zeros((32, 128), F32)], axis=0)
+        ss[i] = jnp.transpose(stat)[0:8]
+
+    def send_state(i):
+        return (
+            remote(cs.at[i], cr.at[i], a_send.at[i], a_recv.at[i], dev_peer(i)),
+            remote(ss.at[i], sr.at[i], st_send.at[i], st_recv.at[i], dev_peer(i)),
+        )
+
+    def attend_step(i, carry):
+        attend(i)
+        for copy in send_state(i):
+            copy.start()
+        return carry
+
+    lax.fori_loop(1, N, attend_step, 0)
+    attend(0)
+    cr[0] = cs[0]
+    sr[0] = ss[0]
+    for i in range(1, N):
+        for copy in send_state(i):
+            copy.wait_recv()
+
+    peaks = jnp.concatenate([sr[i, 0:1] for i in range(N)], axis=0)
+    totals = jnp.concatenate([sr[i, 1:2] for i in range(N)], axis=0)
+    scale = jnp.exp(peaks - jnp.max(peaks, axis=0, keepdims=True))
+    norm = jnp.sum(scale * totals, axis=0, keepdims=True)
+    norm = jnp.where(lax.broadcasted_iota(jnp.int32, (1, 128), 1) < 96, norm, 1.0)
+    factor = jnp.concatenate([scale / norm, jnp.zeros((120, 128), F32)], axis=0)
+    factor = jnp.transpose(factor)
+    context = jnp.zeros((96, 128), F32)
+    for i in range(N):
+        context = context + cr[i].astype(F32) * factor[0:96, i : i + 1]
+    for j in range(6):
+        attn_ref[:, j * 128 : (j + 1) * 128] = context[j * 16 : (j + 1) * 16].astype(BF)
+
+    for b in range(3):
+        out_loads[b].wait()
+
+        def project(n, carry, b=b):
+            cols = pl.ds(pl.multiple_of(n * NT, NT), NT)
+            value = jnp.dot(attn_ref[...], wbuf[b, :, cols], preferred_element_type=F32)
+            po[:, pl.ds(pl.multiple_of(b * hidden + n * NT, NT), NT)] = value.astype(BF)
+            return carry
+
+        lax.fori_loop(0, hidden // NT, project, 0)
+    up_loads[6].start()
+    up_loads[7].start()
+    down_loads[0].start()
+
+    def feat_cols(j):
+        return pl.ds(pl.multiple_of(j * feat, feat), feat)
+
+    def send_partial(i):
+        return remote(
+            po.at[:, feat_cols(lax.rem(d + i, N))], pr.at[i], p_send.at[i], p_recv.at[i], dev_peer(i)
+        )
+
+    for i in range(1, N):
+        send_partial(i).start()
+    mixed = resid[...].astype(F32) + po[:, feat_cols(d)].astype(F32)
+    for i in range(1, N):
+        send_partial(i).wait_recv()
+        mixed = mixed + pr[i].astype(F32)
+    mixed_ref[...] = mixed
+
+    square = jnp.sum(mixed * mixed, axis=1, keepdims=True)
+    high = square.astype(BF).astype(F32)
+    tail_lane = lax.broadcasted_iota(jnp.int32, (16, 128), 1)
+    tail = jnp.where(tail_lane == 0, high, jnp.where(tail_lane == 1, square - high, 0.0))
+    scaled = mixed * gain[:, feat_cols(d)].astype(F32)
+    ext = jnp.concatenate([scaled, tail], axis=1).astype(BF)
+    routed = lax.dot_general(
+        wt_ref[0].astype(BF), ext, (((0,), (0,)), ((), ())), preferred_element_type=F32
+    ).astype(BF)
+    for q in range(G):
+        d1s[q] = routed[q * 16 : (q + 1) * 16]
+
+    def send_routed(i):
+        return remote(
+            d1s.at[lax.rem(g + i, G)], d1r.at[g], e1_send.at[i], e1_recv.at[i], grp_peer(i)
+        )
+
+    for i in range(1, G):
+        send_routed(i).start()
+    d1r[g] = d1s[g]
+    for i in range(1, G):
+        send_routed(i).wait_recv()
+    arrived = [d1r[q].astype(F32) for q in range(G)]
+    for e in range(2):
+        d2s[e] = jnp.concatenate([a[e * 8 : (e + 1) * 8] for a in arrived], axis=0).astype(BF)
+
+    def send_rows(i):
+        return remote(
+            d2s.at[lax.rem(z + i, 4) // 2], xr.at[4 - i], e2_send.at[4 - i], e2_recv.at[4 - i], z_peer(i)
+        )
+
+    def send_core(k):
+        return remote(xr.at[k], xr.at[4 + k], e3_send.at[k], e3_recv.at[k], sibling)
+
+    for i in (2, 1, 3):
+        send_rows(i).start()
+    xr[0] = d2s[z // 2]
+    send_core(0).start()
+
+    def feed(k):
+        gate_loads[k].wait()
+        up_loads[k].wait()
+
+        def tile(n, carry):
+            cols = pl.ds(pl.multiple_of(n * NT, NT), NT)
+            rows = xr[k, :, 0:feat]
+            more_g = jnp.dot(rows, wbuf[3 + k, :, cols], preferred_element_type=F32)
+            more_u = jnp.dot(rows, wbuf[up_slot[k], :, cols], preferred_element_type=F32)
+            if k == 0:
+                acc_g[:, cols] = more_g
+                acc_u[:, cols] = more_u
+            else:
+                acc_g[:, cols] += more_g
+                acc_u[:, cols] += more_u
+            return carry
+
+        lax.fori_loop(0, hidden // NT, tile, 0)
+        if k < 4:
+            down_loads[2 * k + 1].start()
+            down_loads[2 * k + 2].start()
+
+    feed(0)
+    for k in (1, 3, 2):
+        send_rows(4 - k).wait_recv()
+        send_core(k).start()
+    for k in (1, 2, 3):
+        feed(k)
+    for k in range(4):
+        send_core(k).wait_recv()
+    for k in range(4, 8):
+        feed(k)
+
+    squares = jnp.zeros((32, 1), F32)
+    for k in range(8):
+        squares = squares + jnp.sum(xr[k, :, feat:].astype(F32), axis=1, keepdims=True)
+    inv = lax.rsqrt(squares / width + 1e-05)
+    gate_val = acc_g[...] * inv
+    hid[...] = (gate_val / (1.0 + jnp.exp(-gate_val)) * (acc_u[...] * inv)).astype(BF)
+
+    for n in range(9):
+        down_loads[n].wait()
+        col, (start, size) = n // 3, down_rows[n % 3]
+
+        def tile(m, carry, n=n, col=col, start=start, size=size):
+            cols = pl.ds(pl.multiple_of(m * NT, NT), NT)
+            to = pl.ds(pl.multiple_of(col * hidden + m * NT, NT), NT)
+            more = jnp.dot(
+                hid[:, start : start + size],
+                wbuf[down_slot[n], 0:size, cols],
+                preferred_element_type=F32,
+            )
+            if n % 3 == 0:
+                oacc[:, to] = more
+            else:
+                oacc[:, to] += more
+            return carry
+
+        lax.fori_loop(0, hidden // NT, tile, 0)
+
+    def back_core(k):
+        return remote(r1s.at[k], r1r.at[k], b1_send.at[k], b1_recv.at[k], sibling)
+
+    def back_rows(k):
+        return remote(r2s.at[k], r2r.at[k], b2_send.at[k], b2_recv.at[k], z_peer(k))
+
+    def back_group(i):
+        return remote(
+            r3s.at[lax.rem(g + i, G)], r3r.at[g], b3_send.at[i], b3_recv.at[i], grp_peer(i)
+        )
+
+    for k in (2, 1, 3, 0):
+        r1s[k] = oacc[:, feat_cols(chunk_dev(4 + k))].astype(BF)
+        back_core(k).start()
+    for k in (2, 1, 3, 0):
+        back_core(k).wait_recv()
+        value = oacc[:, feat_cols(chunk_dev(k))] + r1r[k].astype(F32)
+        if k:
+            r2s[k] = value.astype(BF)
+            back_rows(k).start()
+    even_share = 1.0 - (z // 2).astype(F32)
+    even = value * even_share
+    odd = value * (1.0 - even_share)
+    for k in range(1, 4):
+        back_rows(k).wait_recv()
+        share = 1.0 - (lax.rem(z - k + 4, 4) // 2).astype(F32)
+        value = r2r[k].astype(F32)
+        even = even + value * share
+        odd = odd + value * (1.0 - share)
+    for q in range(G):
+        r3s[q] = jnp.concatenate([even[q * 8 : q * 8 + 8], odd[q * 8 : q * 8 + 8]], axis=0).astype(BF)
+    for i in range(1, G):
+        back_group(i).start()
+    r3r[g] = r3s[g]
+    for i in range(1, G):
+        back_group(i).wait_recv()
+    rows = jnp.concatenate([r3r[q] for q in range(G)], axis=0)
+    wt_high = wt_ref[1].astype(BF)
+    wt_low = (wt_ref[1] - wt_high.astype(F32)).astype(BF)
+    moe = jnp.dot(wt_high, rows, preferred_element_type=F32) + jnp.dot(
+        wt_low, rows, preferred_element_type=F32
+    )
+    out_ref[...] = (mixed_ref[...] + moe).astype(BF)
+
+    put_k.wait()
+    put_v.wait()
+    for move in moves:
+        move.wait_send()
+    for i in range(1, N):
+        for copy in send_state(i):
+            copy.wait_send()
+        send_partial(i).wait_send()
+    for i in range(1, G):
+        send_routed(i).wait_send()
+        send_rows(i).wait_send()
+        back_rows(i).wait_send()
+        back_group(i).wait_send()
+    for k in range(4):
+        send_core(k).wait_send()
+        back_core(k).wait_send()
+
+
+def fused_layer(
+    cache_k, cache_v, source, lengths, query, new_key, new_value, resid, out_weight, norm_gain,
+    w_gate, w_up, w_down, expert_ids, gate_codes,
+):
+    feat = resid.shape[1]
+    width = query.shape[1]
+    hidden = w_gate.shape[1]
+    ext = feat + 128
+    block = cache_k.shape[1:]
+    vm = pl.BlockSpec(memory_space=pltpu.VMEM)
+    sm = pl.BlockSpec(memory_space=pltpu.SMEM)
+    far = pl.BlockSpec(memory_space=pl.ANY)
+    dma = pltpu.SemaphoreType.DMA
+
+    def buf(shape, kind=BF):
+        return pltpu.VMEM(shape, kind)
+
+    scratch = [
+        buf((16, *block)), buf((16, *block)), buf((6, *block)), buf((6, *block)),
+        buf((6, *block)), buf((6, *block)), buf((16, *block)), buf((16, *block)),
+        buf((96, 16 * block[1]), F32), buf((8, 96, 128)), buf((8, 96, 128)),
+        buf((8, 8, 128), F32), buf((8, 8, 128), F32), buf((16, feat)), buf((16, width)),
+        buf((8, 16, feat)), buf((16, feat), F32),
+        buf((4, 16, ext)), buf((4, 16, ext)), buf((2, 32, ext)), buf((8, 32, ext)),
+        buf((32, hidden), F32), buf((32, hidden), F32), buf((32, hidden)), buf((32, width), F32),
+        buf((4, 32, feat)), buf((4, 32, feat)), buf((4, 32, feat)), buf((4, 32, feat)),
+        buf((4, 16, feat)), buf((4, 16, feat)), buf((2, 16, 64), F32),
+        buf((SLOTS, feat, hidden)), dma((28,)), dma((2,)), dma((2,)),
+        dma((2, 4)), dma((2, 4)), dma((8,)), dma((8,)), dma((8,)), dma((8,)), dma((8,)), dma((8,)),
+        dma((4,)), dma((4,)), dma((4,)), dma((4,)), dma((4,)), dma((4,)),
+        dma((4,)), dma((4,)), dma((4,)), dma((4,)), dma((4,)), dma((4,)),
+    ]
+    return pl.pallas_call(
+        layer_kernel,
+        out_shape=(
+            jax.ShapeDtypeStruct(cache_k.shape, BF),
+            jax.ShapeDtypeStruct(cache_v.shape, BF),
+            jax.ShapeDtypeStruct(resid.shape, BF),
+        ),
+        in_specs=[far, far, sm, sm, vm, vm, vm, vm, far, vm, far, far, far, vm, vm],
+        out_specs=(far, far, vm),
+        scratch_shapes=scratch,
+        compiler_params=pltpu.CompilerParams(
+            collective_id=0, has_side_effects=True, vmem_limit_bytes=(64 << 20) - (256 << 10)
+        ),
+        cost_estimate=pl.CostEstimate(
+            flops=2 * 32 * 3 * width * hidden, bytes_accessed=6 * width * hidden, transcendentals=0
+        ),
+    )(
+        cache_k, cache_v, source, lengths, query, new_key, new_value, resid, out_weight,
+        norm_gain.reshape(1, -1), w_gate, w_up, w_down, expert_ids, gate_codes,
+    )
+
+
+def device_program(*args):
+    cache_k, query, resid, w_gate = args[0], args[4], args[7], args[10]
+    fits = (
+        lax.axis_size("grp") == 4
+        and lax.axis_size("dev") == cache_k.shape[1]
+        and resid.shape[1] * lax.axis_size("dev") == query.shape[1]
+        and w_gate.shape[1] * 3 == query.shape[1]
+        and cache_k.shape[0] == 16
+    )
+    return fused_layer(*args) if fits else on_device(*args)
+
+
 def solution(mesh):
     in_specs = (
         P("grp", None, "dev", None),
@@ -198,5 +683,5 @@
     )
     out_specs = (P("grp", None, "dev", None), P("grp", None, "dev", None), P("grp", "dev"))
     return jax.shard_map(
-        on_device, mesh=mesh, in_specs=in_specs, out_specs=out_specs, check_vma=False
-    )
+        device_program, mesh=mesh, in_specs=in_specs, out_specs=out_specs, check_vma=False
+    )

time: 216 us -> 87.9 us (0.41)
  Pallas kernels: 0 us -> 77 us
  blocking collectives: 60 us -> 0 us
  waiting for transfers between devices: 50.9 us -> 0 us
  matrix products: 40.9 us -> 0 us
  other arithmetic: 16.3 us -> 0 us
  between operations: 14.3 us -> 0.64 us
  starting transfers between devices: 11.3 us -> 0 us
  local copies, waits for them, and re-layouts: 20.7 us -> 9.97 us
    pallas_call x0 -> x1, Pallas kernels: none -> 77 us  [fused_layer(): pl.pallas_call(layer_kernel, out_shape=(jax.ShapeDtypeStruct(cache_k.shap...]
    dot_general x9 -> x0, matrix products: 40.9 us -> none  [the longest x1 20.6 us: expert_ffn(): return jnp.dot(hidden, w_down, preferred_element_type=jnp.float32)]
    all_gather x2 -> x0, blocking collectives: 30 us -> none  [joined(): lax.all_gather(part.astype(kind), axis)]
    reduce_scatter x1 -> x0, waiting for transfers between devices: 29.1 us -> none  [on_device(): lax.psum_scatter(partial_value.astype(jnp.bfloat16), 'dev', scatter_dimen...]
    all_to_all x3 -> x0, waiting for transfers between devices: 21.8 us -> none  [the longest x1 12.9 us: on_device(): lax.all_to_all(back.astype(jnp.bfloat16), ('grp', 'dev'), split_axis=0, c...]
    all_to_all x1 -> x0, blocking collectives: 16.3 us -> none  [on_device(): lax.all_to_all(send_rows, ('grp', 'dev'), split_axis=0, concat_axis=0, ti...]
    psum x1 -> x0, blocking collectives: 13.7 us -> none  [on_device(): total_sq = lax.psum(jnp.sum(mixed * mixed, axis=1), 'dev')]
    all_to_all x3 -> x0, starting transfers between devices: 11.2 us -> none  [the longest x1 5.16 us: on_device(): lax.all_to_all(send_k, 'grp', split_axis=0, concat_axis=0, tiled=True)]
  transfers between devices with their start and end apart: 5 -> 0, of which waited for: 4 -> 0; matrix products, arithmetic and copies ran while one was open for 5% -> 0% of each run, Pallas kernels for 0% -> 0%
where the time goes in v1:
time: 87.9 us; the launch traced here: 87.6 us
  Pallas kernels  77 us (88%)
  local copies, waits for them, and re-layouts  9.97 us (11%)
    pallas_call x1, Pallas kernels, fused_layer(): pl.pallas_call(layer_kernel, out_shape=(jax.ShapeDtypeStruct(cache_k.shap...  77 us
    unnamed x5, local copies, waits for them, and re-layouts  8.64 us

profile of v1, /device:TPU:0, one launch (start us, length us, event | category | flops | bytes accessed | tf_op | source)
XLA Modules:
  0.0 87.6 jit_solution(4905982569982228953)
XLA Ops:
  0.6 1.4 %copy.18.ids_ref = s32[16,2]{1,0:T(8,128)} copy(s32[16,2]{0,1:T(2,128)} %param.28) | data formatting | bytes 256 | tf_op args[13]
  2.0 1.4 %copy.19.codes_ref = s32[16,2]{1,0:T(8,128)} copy(s32[16,2]{0,1:T(2,128)} %param.29) | data formatting | bytes 256 | tf_op args[14]
  3.3 1.3 %reshape.9.gain = bf16[1,6144]{1,0:T(2,128)(2,1)} reshape(bf16[6144]{0:T(1024)(128)(2,1)} %param.24) | data formatting | bytes 24576 | tf_op jit(solution)/shard_map/reshape | solution.py:650
  4.7 77.0 %shard_map.166 = (bf16[16,8,32,128]{3,2,1,0:T(8,128)(2,1)}, bf16[16,8,32,128]{3,2,1,0:T(8,128)(2,1)}, bf16[16,768]{1,0:T(8,128)(2,1)}) custom-call(bf16[16,8,32,128]{3,2,1,0:T(8,128)(2,1)} %ck_hbm.1, bf16[16,8,32,128]{3,2,1,0:T(8,128)(2,1)} %cv_hbm.1, s32[64]{0:T(128)} %source.1, s32[16]{0:T(128)} %lengths.1, bf16[16,6144]{1,0:T(8,128)(2,1)} %query.1, ...), custom_call_target="tpu_custom_call" | custom-call | flops 2415919104 | bytes 75497472 | tf_op jit(solution)/shard_map/pallas_call | solution.py:632
  81.6 2.3 %copy.23 = bf16[16,8,32,128]{3,2,1,0:T(8,128)(2,1)} copy(bf16[16,8,32,128]{3,2,1,0:T(8,128)(2,1)} %get-tuple-element.6) | data formatting | bytes 2097152
  83.9 2.3 %copy.24 = bf16[16,8,32,128]{3,2,1,0:T(8,128)(2,1)} copy(bf16[16,8,32,128]{3,2,1,0:T(8,128)(2,1)} %get-tuple-element.7) | data formatting | bytes 2097152
  86.2 1.3 %copy.25 = bf16[16,768]{1,0:T(8,128)(2,1)} copy(bf16[16,768]{1,0:T(8,128)(2,1)} %get-tuple-element.8) | data formatting | bytes 49152

commit v2 on v1

--- a/solution.py
+++ b/solution.py
@@ -183,8 +183,7 @@
 MESH = pl.DeviceIdType.MESH
 BF = jnp.bfloat16
 F32 = jnp.float32
-SLOTS = 17
-NT = 512
+SLOTS = 16
 
 
 def ask(cond):
@@ -196,7 +195,7 @@
     wg_hbm, wu_hbm, wd_hbm, ids_ref, codes_ref,
     nk_hbm, nv_hbm, out_ref,
     ck, cv, rk, rv, sk, sv, nk, nv,
-    mask_ref, cs, cr, ss, sr, attn_ref, po, pr, mixed_ref,
+    mask_ref, ws, cs, cr, ss, sr, attn_ref, po, pr, mixed_ref,
     d1s, d1r, d2s, xr, acc_g, acc_u, hid, oacc, r1s, r1r, r2s, r2r, r3s, r3r, wt_ref,
     wbuf, wsem, csem, osem,
     ms_send, ms_recv, a_send, a_recv, st_send, st_recv, p_send, p_recv,
@@ -224,7 +223,8 @@
     sibling = (g, z * 2 + 1 - c)
 
     def chunk_dev(k):
-        return lax.rem(z + k % 4, 4) * 2 + (c if k < 4 else 1 - c)
+        other = k // 4
+        return lax.rem(z + k % 4, 4) * 2 + c + other * (1 - 2 * c)
 
     def remote(src, dst, send, recv, to):
         return pltpu.make_async_remote_copy(
@@ -236,29 +236,44 @@
     own_k.start()
     own_v.start()
 
-    def load_rows(hbm, rows, slot, sem):
+    pair = 2 * feat
+
+    def pair_cols(k):
+        return pl.ds(pl.multiple_of(lax.rem(z + k, 4) * pair, pair), pair)
+
+    def gate_slot(k):
+        return 4 + k
+
+    def up_slot(k):
+        return lax.rem(12 + k, SLOTS)
+
+    def down_slot(n):
+        return (4 + n // 2) * (1 - n % 2) + lax.rem(12 + n // 2, SLOTS) * (n % 2)
+
+    def load_rows(hbm, k, slot, sem):
+        rows = pl.ds(pl.multiple_of(chunk_dev(k) * feat, feat), feat)
+        return pltpu.make_async_copy(hbm.at[rows], wbuf.at[slot], wsem.at[sem])
+
+    def load_gate(k):
+        return load_rows(wg_hbm, k, gate_slot(k), 4 + k)
+
+    def load_up(k):
+        return load_rows(wu_hbm, k, up_slot(k), 12 + k)
+
+    def load_out(b):
+                return pltpu.make_async_copy(
+            ow_hbm.at[:, pair_cols(b + 1)], wbuf.at[b, :, pl.ds(0, pair)], wsem.at[b]
+        )
+
+    down_rows = [(0, feat), (feat, feat), (2 * feat, hidden - 2 * feat)]
+
+    def load_down(t, r):
+        start, size = down_rows[r]
+        n = 3 * t + r
         return pltpu.make_async_copy(
-            hbm.at[pl.ds(pl.multiple_of(rows, feat), feat)], wbuf.at[slot], wsem.at[sem]
-        )
-
-    out_loads = [
-        pltpu.make_async_copy(ow_hbm.at[:, pl.ds(b * hidden, hidden)], wbuf.at[b], wsem.at[b])
-        for b in range(3)
-    ]
-    gate_loads = [load_rows(wg_hbm, chunk_dev(k) * feat, 3 + k, 3 + k) for k in range(8)]
-    up_slot = [11, 12, 13, 14, 15, 16, 0, 1]
-    up_loads = [load_rows(wu_hbm, chunk_dev(k) * feat, up_slot[k], 11 + k) for k in range(8)]
-    down_slot = [2, 3, 11, 4, 12, 5, 13, 6, 14]
-    down_rows = [(0, feat), (feat, feat), (2 * feat, hidden - 2 * feat)]
-    down_loads = []
-    for n in range(9):
-        col, (start, size) = n // 3, down_rows[n % 3]
-        down_loads.append(
-            pltpu.make_async_copy(
-                wd_hbm.at[pl.ds(start, size), pl.ds(col * hidden, hidden)],
-                wbuf.at[down_slot[n], pl.ds(0, size)],
-                wsem.at[19 + n],
-            )
+            wd_hbm.at[pl.ds(start, size), pair_cols(t + 1)],
+            wbuf.at[down_slot(n), pl.ds(0, size), pl.ds(0, pair)],
+            wsem.at[20 + n],
         )
 
     barrier = pltpu.get_barrier_semaphore()
@@ -266,12 +281,12 @@
         pl.semaphore_signal(barrier, inc=1, device_id=grp_peer(i), device_id_type=MESH)
     for i in range(1, N):
         pl.semaphore_signal(barrier, inc=1, device_id=dev_peer(i), device_id_type=MESH)
-    for load in out_loads:
-        load.start()
+    for b in range(4):
+        load_out(b).start()
     for k in range(8):
-        gate_loads[k].start()
-        if k < 6:
-            up_loads[k].start()
+        load_gate(k).start()
+        if k < 4:
+            load_up(k).start()
 
     zero = jnp.int32(0)
     own_k.wait()
@@ -294,9 +309,9 @@
     pl.semaphore_wait(barrier, G - 1 + N - 1)
 
     moves = []
-    for i in range(1, G):
-        part = pl.ds(2 * (i - 1), 2)
-        for t, (src, dst) in enumerate(((sk, rk), (sv, rv))):
+    for t, (src, dst) in enumerate(((sk, rk), (sv, rv))):
+        for i in range(1, G):
+            part = pl.ds(2 * (i - 1), 2)
             move = remote(
                 src.at[part], dst.at[part], ms_send.at[t, i], ms_recv.at[t, i], grp_peer(i)
             )
@@ -311,26 +326,24 @@
     inside = (d * block_len + lane % block_len <= limit) & (lane // block_len == row % 16)
     mask_ref[...] = jnp.where(inside, 1.0, 0.0)
 
-    expert_of = lax.broadcasted_iota(jnp.int32, (16, 64), 1) // 8
-    slot_of = lax.broadcasted_iota(jnp.int32, (16, 64), 1) % 8
+    expert_of = lax.broadcasted_iota(jnp.int32, (64, 16), 0) // 8
+    slot_of = lax.broadcasted_iota(jnp.int32, (64, 16), 0) % 8
     codes = codes_ref[...].astype(F32)
-    total_code = codes[:, 0:1] + codes[:, 1:2]
-    hot0 = jnp.where(ids_ref[:, 0:1] == expert_of, 1.0, 0.0)
-    hot1 = jnp.where(ids_ref[:, 1:2] == expert_of, 1.0, 0.0)
+    total_code = codes[0:1] + codes[1:2]
+    hot0 = jnp.where(ids_ref[0:1, :] == expert_of, 1.0, 0.0)
+    hot1 = jnp.where(ids_ref[1:2, :] == expert_of, 1.0, 0.0)
     hot = hot0 + hot1
     t_row = lax.broadcasted_iota(jnp.int32, (16, 16), 0)
     t_col = lax.broadcasted_iota(jnp.int32, (16, 16), 1)
-    lower = jnp.where(t_col < t_row, 1.0, 0.0).astype(BF)
-    rank = jnp.dot(lower, hot.astype(BF), preferred_element_type=F32)
+    upper = jnp.where(t_row < t_col, 1.0, 0.0).astype(BF)
+    rank = jnp.dot(hot.astype(BF), upper, preferred_element_type=F32)
     placed = jnp.where(rank == slot_of.astype(F32), 1.0, 0.0)
     wt_ref[0] = hot * placed
-    wt_ref[1] = (hot0 * (codes[:, 0:1] / total_code) + hot1 * (codes[:, 1:2] / total_code)) * placed
-
-    for move in moves:
-        move.wait_recv()
+    wt_ref[1] = (hot0 * (codes[0:1] / total_code) + hot1 * (codes[1:2] / total_code)) * placed
 
     counts = [zero] * G
     p_iota = lax.broadcasted_iota(jnp.int32, (8, block_len, 128), 1)
+    places = []
     for s in range(16):
         origin = source[g * 16 + s] // 16
         off = lax.rem(g - origin + G, G)
@@ -339,39 +352,58 @@
             here = ask(off == i)
             at = at + here * (2 * (i - 1) + counts[i])
             counts[i] = counts[i] + here
-        at = jnp.minimum(at, 5)
-        stays = jnp.full((8, block_len, 128), off, jnp.int32) == 0
-        hit = p_iota == lengths[s] - d * block_len
-        for own, got, new, dst in ((ck, rk, new_key, nk), (cv, rv, new_value, nv)):
+        places.append((off, jnp.minimum(at, 5)))
+
+    def build(own, got, new, dst):
+        for s, (off, at) in enumerate(places):
+            stays = jnp.full((8, block_len, 128), off, jnp.int32) == 0
+            hit = p_iota == lengths[s] - d * block_len
             kept = jnp.where(stays, own[s].astype(F32), got[at].astype(F32))
             fresh = jnp.broadcast_to(new[s].astype(F32)[:, None, :], (8, block_len, 128))
             dst[s] = jnp.where(hit, fresh, kept).astype(BF)
 
+    for move in moves[: G - 1]:
+        move.wait_recv()
+    build(ck, rk, new_key, nk)
     put_k = pltpu.make_async_copy(nk, nk_hbm, osem.at[0])
     put_v = pltpu.make_async_copy(nv, nv_hbm, osem.at[1])
     put_k.start()
-    put_v.start()
 
     stat_lane = lax.broadcasted_iota(jnp.int32, (96, 128), 1)
 
-    def attend(i):
+    def score(i):
         h = lax.rem(d + i, N)
         rows = [
             query[:, pl.ds(pl.multiple_of((h * 6 + j) * 128, 128), 128)] for j in range(6)
         ]
         q_h = jnp.concatenate(rows, axis=0)
         k_h = nk[:, pl.ds(h, 1)].reshape(16 * block_len, 128)
-        v_h = nv[:, pl.ds(h, 1)].reshape(16 * block_len, 128)
         valid = mask_ref[...] > 0.5
         scores = lax.dot_general(q_h, k_h, (((1,), (1,)), ((), ())), preferred_element_type=F32)
         scores = jnp.where(valid, scores / 128**0.5, F32(-1e30))
         peak = jnp.max(scores, axis=1, keepdims=True)
         weights = jnp.where(valid, jnp.exp(scores - peak), 0.0)
         total = jnp.sum(weights, axis=1, keepdims=True)
-        cs[i] = jnp.dot(weights.astype(BF), v_h, preferred_element_type=F32).astype(BF)
+        ws[i] = weights.astype(BF)
         stat = jnp.where(stat_lane == 0, peak, jnp.where(stat_lane == 1, total, 0.0))
         stat = jnp.concatenate([stat, jnp.zeros((32, 128), F32)], axis=0)
         ss[i] = jnp.transpose(stat)[0:8]
+
+    def score_step(m, carry):
+        score(2 * m)
+        score(2 * m + 1)
+        return carry
+
+    lax.fori_loop(0, N // 2, score_step, 0)
+
+    def attend(i):
+        v_h = nv[:, pl.ds(lax.rem(d + i, N), 1)].reshape(16 * block_len, 128)
+        cs[i] = jnp.dot(ws[i], v_h, preferred_element_type=F32).astype(BF)
+
+    for move in moves[G - 1 :]:
+        move.wait_recv()
+    build(cv, rv, new_value, nv)
+    put_v.start()
 
     def send_state(i):
         return (
@@ -385,7 +417,8 @@
             copy.start()
         return carry
 
-    lax.fori_loop(1, N, attend_step, 0)
+    for i in range(1, N):
+        attend_step(i, 0)
     attend(0)
     cr[0] = cs[0]
     sr[0] = ss[0]
@@ -406,34 +439,45 @@
     for j in range(6):
         attn_ref[:, j * 128 : (j + 1) * 128] = context[j * 16 : (j + 1) * 16].astype(BF)
 
-    for b in range(3):
-        out_loads[b].wait()
-
-        def project(n, carry, b=b):
-            cols = pl.ds(pl.multiple_of(n * NT, NT), NT)
-            value = jnp.dot(attn_ref[...], wbuf[b, :, cols], preferred_element_type=F32)
-            po[:, pl.ds(pl.multiple_of(b * hidden + n * NT, NT), NT)] = value.astype(BF)
-            return carry
-
-        lax.fori_loop(0, hidden // NT, project, 0)
-    up_loads[6].start()
-    up_loads[7].start()
-    down_loads[0].start()
-
     def feat_cols(j):
         return pl.ds(pl.multiple_of(j * feat, feat), feat)
 
-    def send_partial(i):
+    def send_partial(k, core):
+        at = 2 * k + core
         return remote(
-            po.at[:, feat_cols(lax.rem(d + i, N))], pr.at[i], p_send.at[i], p_recv.at[i], dev_peer(i)
-        )
-
-    for i in range(1, N):
-        send_partial(i).start()
-    mixed = resid[...].astype(F32) + po[:, feat_cols(d)].astype(F32)
-    for i in range(1, N):
-        send_partial(i).wait_recv()
-        mixed = mixed + pr[i].astype(F32)
+            po.at[k, :, feat_cols(core)],
+            pr.at[2 * k + c],
+            p_send.at[at],
+            p_recv.at[2 * k + c],
+            (g, lax.rem(z + k, 4) * 2 + core),
+        )
+
+    def core_partial():
+        return remote(po.at[0, :, feat_cols(1 - c)], pr.at[0], p_send.at[0], p_recv.at[0], sibling)
+
+    for b in range(4):
+        load_out(b).wait()
+        k = (b + 1) % 4
+        value = jnp.dot(
+            attn_ref[...], wbuf[b, :, 0:pair], preferred_element_type=F32
+        )
+        po[k] = value.astype(BF)
+        if k:
+            send_partial(k, 0).start()
+            send_partial(k, 1).start()
+        else:
+            core_partial().start()
+    for k in range(4, 8):
+        load_up(k).start()
+
+    mixed = resid[...].astype(F32) + po[0, :, feat_cols(c)].astype(F32)
+    core_partial().wait_recv()
+    mixed = mixed + pr[0].astype(F32)
+    for at in range(2, N):
+        remote(
+            po.at[0, :, feat_cols(0)], pr.at[at], p_send.at[1], p_recv.at[at], sibling
+        ).wait_recv()
+        mixed = mixed + pr[at].astype(F32)
     mixed_ref[...] = mixed
 
     square = jnp.sum(mixed * mixed, axis=1, keepdims=True)
@@ -443,7 +487,7 @@
     scaled = mixed * gain[:, feat_cols(d)].astype(F32)
     ext = jnp.concatenate([scaled, tail], axis=1).astype(BF)
     routed = lax.dot_general(
-        wt_ref[0].astype(BF), ext, (((0,), (0,)), ((), ())), preferred_element_type=F32
+        wt_ref[0].astype(BF), ext, (((1,), (0,)), ((), ())), preferred_element_type=F32
     ).astype(BF)
     for q in range(G):
         d1s[q] = routed[q * 16 : (q + 1) * 16]
@@ -476,37 +520,40 @@
     send_core(0).start()
 
     def feed(k):
-        gate_loads[k].wait()
-        up_loads[k].wait()
-
-        def tile(n, carry):
-            cols = pl.ds(pl.multiple_of(n * NT, NT), NT)
-            rows = xr[k, :, 0:feat]
-            more_g = jnp.dot(rows, wbuf[3 + k, :, cols], preferred_element_type=F32)
-            more_u = jnp.dot(rows, wbuf[up_slot[k], :, cols], preferred_element_type=F32)
-            if k == 0:
-                acc_g[:, cols] = more_g
-                acc_u[:, cols] = more_u
-            else:
-                acc_g[:, cols] += more_g
-                acc_u[:, cols] += more_u
-            return carry
-
-        lax.fori_loop(0, hidden // NT, tile, 0)
-        if k < 4:
-            down_loads[2 * k + 1].start()
-            down_loads[2 * k + 2].start()
+        load_gate(k).wait()
+        load_up(k).wait()
+        rows = xr[k, :, 0:feat]
+        value_g = jnp.dot(rows, wbuf[gate_slot(k)], preferred_element_type=F32)
+        value_u = jnp.dot(rows, wbuf[up_slot(k)], preferred_element_type=F32)
+        if isinstance(k, int):
+            acc_g[...] = value_g
+            acc_u[...] = value_u
+        else:
+            acc_g[...] += value_g
+            acc_u[...] += value_u
+
+    def feed_step(k, carry):
+        feed(k)
+        return carry
+
+    def start_downs(k):
+        for n in (2 * k, 2 * k + 1):
+            load_down(n // 3, n % 3).start()
 
     feed(0)
+    start_downs(0)
     for k in (1, 3, 2):
         send_rows(4 - k).wait_recv()
         send_core(k).start()
-    for k in (1, 2, 3):
-        feed(k)
+    lax.fori_loop(1, 4, feed_step, 0)
+    for k in range(1, 4):
+        start_downs(k)
     for k in range(4):
         send_core(k).wait_recv()
-    for k in range(4, 8):
-        feed(k)
+    lax.fori_loop(4, 6, feed_step, 0)
+    for k in range(4, 6):
+        start_downs(k)
+    lax.fori_loop(6, 8, feed_step, 0)
 
     squares = jnp.zeros((32, 1), F32)
     for k in range(8):
@@ -515,53 +562,50 @@
     gate_val = acc_g[...] * inv
     hid[...] = (gate_val / (1.0 + jnp.exp(-gate_val)) * (acc_u[...] * inv)).astype(BF)
 
-    for n in range(9):
-        down_loads[n].wait()
-        col, (start, size) = n // 3, down_rows[n % 3]
-
-        def tile(m, carry, n=n, col=col, start=start, size=size):
-            cols = pl.ds(pl.multiple_of(m * NT, NT), NT)
-            to = pl.ds(pl.multiple_of(col * hidden + m * NT, NT), NT)
-            more = jnp.dot(
-                hid[:, start : start + size],
-                wbuf[down_slot[n], 0:size, cols],
-                preferred_element_type=F32,
-            )
-            if n % 3 == 0:
-                oacc[:, to] = more
-            else:
-                oacc[:, to] += more
-            return carry
-
-        lax.fori_loop(0, hidden // NT, tile, 0)
-
     def back_core(k):
         return remote(r1s.at[k], r1r.at[k], b1_send.at[k], b1_recv.at[k], sibling)
 
     def back_rows(k):
-        return remote(r2s.at[k], r2r.at[k], b2_send.at[k], b2_recv.at[k], z_peer(k))
+        return remote(r2s.at[k], r2r.at[k], b2_send.at[k], b2_recv.at[k], z_peer(k + 1))
 
     def back_group(i):
         return remote(
             r3s.at[lax.rem(g + i, G)], r3r.at[g], b3_send.at[i], b3_recv.at[i], grp_peer(i)
         )
 
-    for k in (2, 1, 3, 0):
-        r1s[k] = oacc[:, feat_cols(chunk_dev(4 + k))].astype(BF)
-        back_core(k).start()
-    for k in (2, 1, 3, 0):
-        back_core(k).wait_recv()
-        value = oacc[:, feat_cols(chunk_dev(k))] + r1r[k].astype(F32)
-        if k:
-            r2s[k] = value.astype(BF)
-            back_rows(k).start()
+    def expand(t):
+        value = jnp.zeros((32, pair), F32)
+        for r, (start, size) in enumerate(down_rows):
+            load_down(t, r).wait()
+            value = value + jnp.dot(
+                hid[:, start : start + size],
+                wbuf[down_slot(3 * t + r), 0:size, 0:pair],
+                preferred_element_type=F32,
+            )
+        oacc[t] = value
+        r1s[t] = oacc[t, :, feat_cols(1 - c)].astype(BF)
+        back_core(t).start()
+
+    def joined_share(t):
+        back_core(t).wait_recv()
+        return oacc[t, :, feat_cols(c)] + r1r[t].astype(F32)
+
+    def expand_step(t, carry):
+        expand(t)
+        r2s[t - 1] = joined_share(t - 1).astype(BF)
+        back_rows(t - 1).start()
+        return carry
+
+    expand(0)
+    lax.fori_loop(1, 4, expand_step, 0)
+    value = joined_share(3)
     even_share = 1.0 - (z // 2).astype(F32)
     even = value * even_share
     odd = value * (1.0 - even_share)
-    for k in range(1, 4):
-        back_rows(k).wait_recv()
-        share = 1.0 - (lax.rem(z - k + 4, 4) // 2).astype(F32)
-        value = r2r[k].astype(F32)
+    for t in range(3):
+        back_rows(t).wait_recv()
+        share = 1.0 - (lax.rem(z - t + 3, 4) // 2).astype(F32)
+        value = r2r[t].astype(F32)
         even = even + value * share
         odd = odd + value * (1.0 - share)
     for q in range(G):
@@ -574,8 +618,9 @@
     rows = jnp.concatenate([r3r[q] for q in range(G)], axis=0)
     wt_high = wt_ref[1].astype(BF)
     wt_low = (wt_ref[1] - wt_high.astype(F32)).astype(BF)
-    moe = jnp.dot(wt_high, rows, preferred_element_type=F32) + jnp.dot(
-        wt_low, rows, preferred_element_type=F32
+    moe = sum(
+        lax.dot_general(part, rows, (((0,), (0,)), ((), ())), preferred_element_type=F32)
+        for part in (wt_high, wt_low)
     )
     out_ref[...] = (mixed_ref[...] + moe).astype(BF)
 
@@ -586,15 +631,31 @@
     for i in range(1, N):
         for copy in send_state(i):
             copy.wait_send()
-        send_partial(i).wait_send()
+    core_partial().wait_send()
+    for k in range(1, 4):
+        send_partial(k, 0).wait_send()
+        send_partial(k, 1).wait_send()
     for i in range(1, G):
         send_routed(i).wait_send()
         send_rows(i).wait_send()
-        back_rows(i).wait_send()
+        back_rows(i - 1).wait_send()
         back_group(i).wait_send()
     for k in range(4):
         send_core(k).wait_send()
         back_core(k).wait_send()
+
+
+def hand_over(k_in, v_in, out_in, k_out, v_out, out_out, sems):
+    copies = [pltpu.make_async_copy(out_in, out_out, sems.at[8])]
+    quarter = k_in.shape[0] // 4
+    for n in range(4):
+        part = pl.ds(n * quarter, quarter)
+        copies.append(pltpu.make_async_copy(k_in.at[part], k_out.at[part], sems.at[2 * n]))
+        copies.append(pltpu.make_async_copy(v_in.at[part], v_out.at[part], sems.at[2 * n + 1]))
+    for copy in copies:
+        copy.start()
+    for copy in copies:
+        copy.wait()
 
 
 def fused_layer(
@@ -617,19 +678,19 @@
     scratch = [
         buf((16, *block)), buf((16, *block)), buf((6, *block)), buf((6, *block)),
         buf((6, *block)), buf((6, *block)), buf((16, *block)), buf((16, *block)),
-        buf((96, 16 * block[1]), F32), buf((8, 96, 128)), buf((8, 96, 128)),
-        buf((8, 8, 128), F32), buf((8, 8, 128), F32), buf((16, feat)), buf((16, width)),
+        buf((96, 16 * block[1]), F32), buf((8, 96, 16 * block[1])), buf((8, 96, 128)), buf((8, 96, 128)),
+        buf((8, 8, 128), F32), buf((8, 8, 128), F32), buf((16, feat)), buf((4, 16, 2 * feat)),
         buf((8, 16, feat)), buf((16, feat), F32),
         buf((4, 16, ext)), buf((4, 16, ext)), buf((2, 32, ext)), buf((8, 32, ext)),
-        buf((32, hidden), F32), buf((32, hidden), F32), buf((32, hidden)), buf((32, width), F32),
+        buf((32, hidden), F32), buf((32, hidden), F32), buf((32, hidden)), buf((4, 32, 2 * feat), F32),
         buf((4, 32, feat)), buf((4, 32, feat)), buf((4, 32, feat)), buf((4, 32, feat)),
-        buf((4, 16, feat)), buf((4, 16, feat)), buf((2, 16, 64), F32),
-        buf((SLOTS, feat, hidden)), dma((28,)), dma((2,)), dma((2,)),
+        buf((4, 16, feat)), buf((4, 16, feat)), buf((2, 64, 16), F32),
+        buf((SLOTS, feat, hidden)), dma((32,)), dma((2,)), dma((2,)),
         dma((2, 4)), dma((2, 4)), dma((8,)), dma((8,)), dma((8,)), dma((8,)), dma((8,)), dma((8,)),
         dma((4,)), dma((4,)), dma((4,)), dma((4,)), dma((4,)), dma((4,)),
         dma((4,)), dma((4,)), dma((4,)), dma((4,)), dma((4,)), dma((4,)),
     ]
-    return pl.pallas_call(
+    results = pl.pallas_call(
         layer_kernel,
         out_shape=(
             jax.ShapeDtypeStruct(cache_k.shape, BF),
@@ -647,8 +708,16 @@
         ),
     )(
         cache_k, cache_v, source, lengths, query, new_key, new_value, resid, out_weight,
-        norm_gain.reshape(1, -1), w_gate, w_up, w_down, expert_ids, gate_codes,
-    )
+        norm_gain.reshape(1, -1), w_gate, w_up, w_down, expert_ids.T, gate_codes.T,
+    )
+    return pl.pallas_call(
+        hand_over,
+        out_shape=tuple(jax.ShapeDtypeStruct(r.shape, r.dtype) for r in results),
+        in_specs=[far] * 3,
+        out_specs=(far,) * 3,
+        scratch_shapes=[dma((9,))],
+        cost_estimate=pl.CostEstimate(flops=0, bytes_accessed=8 << 20, transcendentals=0),
+    )(*results)
 
 
 def device_program(*args):

time: 87.9 us -> 134 us (1.52)
  Pallas kernels: 77 us -> 131 us
  local copies, waits for them, and re-layouts: 9.97 us -> 1.33 us
    pallas_call x0 -> x1, Pallas kernels: none -> 65.5 us  [fused_layer(): pl.pallas_call(hand_over, out_shape=tuple((jax.ShapeDtypeStruct(r.shape,...]
    pallas_call x1, Pallas kernels: 77 us -> 65.9 us  [fused_layer(): pl.pallas_call(layer_kernel, out_shape=(jax.ShapeDtypeStruct(cache_k.shap...]
    unnamed x5 -> x0, local copies, waits for them, and re-layouts: 8.64 us -> none
where the time goes in v2:
time: 134 us; the launch traced here: 133 us
  Pallas kernels  131 us (98%)
    pallas_call x1, Pallas kernels, fused_layer(): pl.pallas_call(layer_kernel, out_shape=(jax.ShapeDtypeStruct(cache_k.shap...  65.9 us
    pallas_call x1, Pallas kernels, fused_layer(): pl.pallas_call(hand_over, out_shape=tuple((jax.ShapeDtypeStruct(r.shape,...  65.5 us

profile of v2, /device:TPU:0, one launch (start us, length us, event | category | flops | bytes accessed | tf_op | source)
XLA Modules:
  0.0 133.3 jit_solution(10094105074408477541)
XLA Ops:
  0.6 1.3 reshape.9.gain
  2.0 65.9 %shard_map.166 = (bf16[16,8,32,128]{3,2,1,0:T(8,128)(2,1)}, bf16[16,8,32,128]{3,2,1,0:T(8,128)(2,1)}, bf16[16,768]{1,0:T(8,128)(2,1)}) custom-call(bf16[16,8,32,128]{3,2,1,0:T(8,128)(2,1)} %ck_hbm.1, bf16[16,8,32,128]{3,2,1,0:T(8,128)(2,1)} %cv_hbm.1, s32[64]{0:T(128)} %source.1, s32[16]{0:T(128)} %lengths.1, bf16[16,6144]{1,0:T(8,128)(2,1)} %query.1, ...), custom_call_target="tpu_custom_call" | custom-call | flops 2415919104 | bytes 75497472 | tf_op jit(solution)/shard_map/pallas_call | solution.py:693
  67.9 65.5 %shard_map.167 = (bf16[16,8,32,128]{3,2,1,0:T(8,128)(2,1)}, bf16[16,8,32,128]{3,2,1,0:T(8,128)(2,1)}, bf16[16,768]{1,0:T(8,128)(2,1)}) custom-call(bf16[16,8,32,128]{3,2,1,0:T(8,128)(2,1)} %get-tuple-element.6.k_in, bf16[16,8,32,128]{3,2,1,0:T(8,128)(2,1)} %get-tuple-element.7.v_in, bf16[16,768]{1,0:T(8,128)(2,1)} %get-tuple-element.8.out_in), custom_call_target="tpu_custom_call" | custom-call | bytes 8388608 | tf_op jit(solution)/shard_map/pallas_call | solution.py:713

commit v3 on v2

--- a/solution.py
+++ b/solution.py
@@ -254,11 +254,13 @@
         rows = pl.ds(pl.multiple_of(chunk_dev(k) * feat, feat), feat)
         return pltpu.make_async_copy(hbm.at[rows], wbuf.at[slot], wsem.at[sem])
 
-    def load_gate(k):
-        return load_rows(wg_hbm, k, gate_slot(k), 4 + k)
-
-    def load_up(k):
-        return load_rows(wu_hbm, k, up_slot(k), 12 + k)
+    order = (0, 4, 1, 3, 2, 5, 7, 6)
+
+    def load_gate(p, k):
+        return load_rows(wg_hbm, k, gate_slot(p), 4 + p)
+
+    def load_up(p, k):
+        return load_rows(wu_hbm, k, up_slot(p), 12 + p)
 
     def load_out(b):
                 return pltpu.make_async_copy(
@@ -283,10 +285,10 @@
         pl.semaphore_signal(barrier, inc=1, device_id=dev_peer(i), device_id_type=MESH)
     for b in range(4):
         load_out(b).start()
-    for k in range(8):
-        load_gate(k).start()
-        if k < 4:
-            load_up(k).start()
+    for p, k in enumerate(order):
+        load_gate(p, k).start()
+        if p < 4:
+            load_up(p, k).start()
 
     zero = jnp.int32(0)
     own_k.wait()
@@ -467,8 +469,8 @@
             send_partial(k, 1).start()
         else:
             core_partial().start()
-    for k in range(4, 8):
-        load_up(k).start()
+    for p in range(4, 8):
+        load_up(p, order[p]).start()
 
     mixed = resid[...].astype(F32) + po[0, :, feat_cols(c)].astype(F32)
     core_partial().wait_recv()
@@ -484,7 +486,7 @@
     high = square.astype(BF).astype(F32)
     tail_lane = lax.broadcasted_iota(jnp.int32, (16, 128), 1)
     tail = jnp.where(tail_lane == 0, high, jnp.where(tail_lane == 1, square - high, 0.0))
-    scaled = mixed * gain[:, feat_cols(d)].astype(F32)
+    scaled = mixed * gain[feat_cols(d)].astype(F32).reshape(1, feat)
     ext = jnp.concatenate([scaled, tail], axis=1).astype(BF)
     routed = lax.dot_general(
         wt_ref[0].astype(BF), ext, (((1,), (0,)), ((), ())), preferred_element_type=F32
@@ -519,41 +521,37 @@
     xr[0] = d2s[z // 2]
     send_core(0).start()
 
-    def feed(k):
-        load_gate(k).wait()
-        load_up(k).wait()
-        rows = xr[k, :, 0:feat]
-        value_g = jnp.dot(rows, wbuf[gate_slot(k)], preferred_element_type=F32)
-        value_u = jnp.dot(rows, wbuf[up_slot(k)], preferred_element_type=F32)
-        if isinstance(k, int):
-            acc_g[...] = value_g
-            acc_u[...] = value_u
-        else:
-            acc_g[...] += value_g
-            acc_u[...] += value_u
-
-    def feed_step(k, carry):
-        feed(k)
-        return carry
-
-    def start_downs(k):
-        for n in (2 * k, 2 * k + 1):
-            load_down(n // 3, n % 3).start()
-
-    feed(0)
-    start_downs(0)
-    for k in (1, 3, 2):
+    acc_g[...] = jnp.zeros(acc_g.shape, F32)
+    acc_u[...] = jnp.zeros(acc_u.shape, F32)
+
+    def feed_two(p, first, second):
+        def feed(n, carry):
+            k = first + n * (second - first)
+            load_gate(p + n, k).wait()
+            load_up(p + n, k).wait()
+            rows = xr[k, :, 0:feat]
+            acc_g[...] += jnp.dot(rows, wbuf[gate_slot(p + n)], preferred_element_type=F32)
+            acc_u[...] += jnp.dot(rows, wbuf[up_slot(p + n)], preferred_element_type=F32)
+            return carry
+
+        lax.fori_loop(0, 2, feed, 0)
+        if p < 6:
+            for n in range(2 * p, 2 * p + 4):
+                load_down(n // 3, n % 3).start()
+
+    send_core(0).wait_recv()
+    feed_two(0, 0, 4)
+    for k in (1, 3):
         send_rows(4 - k).wait_recv()
         send_core(k).start()
-    lax.fori_loop(1, 4, feed_step, 0)
-    for k in range(1, 4):
-        start_downs(k)
-    for k in range(4):
-        send_core(k).wait_recv()
-    lax.fori_loop(4, 6, feed_step, 0)
-    for k in range(4, 6):
-        start_downs(k)
-    lax.fori_loop(6, 8, feed_step, 0)
+    feed_two(2, 1, 3)
+    send_rows(2).wait_recv()
+    send_core(2).start()
+    send_core(1).wait_recv()
+    feed_two(4, 2, 5)
+    send_core(3).wait_recv()
+    send_core(2).wait_recv()
+    feed_two(6, 7, 6)
 
     squares = jnp.zeros((32, 1), F32)
     for k in range(8):
@@ -645,16 +643,25 @@
         back_core(k).wait_send()
 
 
-def hand_over(k_in, v_in, out_in, k_out, v_out, out_out, sems):
-    copies = [pltpu.make_async_copy(out_in, out_out, sems.at[8])]
+def hand_over(k_in, v_in, out_in, k_out, v_out, out_out, k_mid, v_mid, out_mid, in_sems, out_sems):
+    stages = [(out_in, out_mid, out_out)]
     quarter = k_in.shape[0] // 4
     for n in range(4):
         part = pl.ds(n * quarter, quarter)
-        copies.append(pltpu.make_async_copy(k_in.at[part], k_out.at[part], sems.at[2 * n]))
-        copies.append(pltpu.make_async_copy(v_in.at[part], v_out.at[part], sems.at[2 * n + 1]))
-    for copy in copies:
+        stages.append((k_in.at[part], k_mid.at[part], k_out.at[part]))
+        stages.append((v_in.at[part], v_mid.at[part], v_out.at[part]))
+    first = [
+        pltpu.make_async_copy(src, mid, in_sems.at[n]) for n, (src, mid, _) in enumerate(stages)
+    ]
+    second = [
+        pltpu.make_async_copy(mid, dst, out_sems.at[n]) for n, (_, mid, dst) in enumerate(stages)
+    ]
+    for copy in first:
         copy.start()
-    for copy in copies:
+    for came, goes in zip(first, second):
+        came.wait()
+        goes.start()
+    for copy in second:
         copy.wait()
 
 
@@ -708,14 +715,14 @@
         ),
     )(
         cache_k, cache_v, source, lengths, query, new_key, new_value, resid, out_weight,
-        norm_gain.reshape(1, -1), w_gate, w_up, w_down, expert_ids.T, gate_codes.T,
+        norm_gain, w_gate, w_up, w_down, expert_ids.T, gate_codes.T,
     )
     return pl.pallas_call(
         hand_over,
         out_shape=tuple(jax.ShapeDtypeStruct(r.shape, r.dtype) for r in results),
         in_specs=[far] * 3,
         out_specs=(far,) * 3,
-        scratch_shapes=[dma((9,))],
+        scratch_shapes=[buf(r.shape) for r in results] + [dma((9,)), dma((9,))],
         cost_estimate=pl.CostEstimate(flops=0, bytes_accessed=8 << 20, transcendentals=0),
     )(*results)
 

time: 134 us -> 67.8 us (0.51)
  Pallas kernels: 131 us -> 67 us
    pallas_call x1, Pallas kernels: 65.5 us -> 2.43 us  [fused_layer(): pl.pallas_call(hand_over, out_shape=tuple((jax.ShapeDtypeStruct(r.shape,...]
where the time goes in v3:
time: 67.8 us; the launch traced here: 67.6 us
  Pallas kernels  67 us (99%)
    pallas_call x1, Pallas kernels, fused_layer(): pl.pallas_call(layer_kernel, out_shape=(jax.ShapeDtypeStruct(cache_k.shap...  64.6 us
    pallas_call x1, Pallas kernels, fused_layer(): pl.pallas_call(hand_over, out_shape=tuple((jax.ShapeDtypeStruct(r.shape,...  2.43 us

profile of v3, /device:TPU:0, one launch (start us, length us, event | category | flops | bytes accessed | tf_op | source)
XLA Modules:
  0.0 67.6 jit_solution(1593829554870619883)
XLA Ops:
  0.6 64.6 %shard_map.166 = (bf16[16,8,32,128]{3,2,1,0:T(8,128)(2,1)}, bf16[16,8,32,128]{3,2,1,0:T(8,128)(2,1)}, bf16[16,768]{1,0:T(8,128)(2,1)}) custom-call(bf16[16,8,32,128]{3,2,1,0:T(8,128)(2,1)} %ck_hbm.1, bf16[16,8,32,128]{3,2,1,0:T(8,128)(2,1)} %cv_hbm.1, s32[64]{0:T(128)} %source.1, s32[16]{0:T(128)} %lengths.1, bf16[16,6144]{1,0:T(8,128)(2,1)} %query.1, ...), custom_call_target="tpu_custom_call" | custom-call | flops 2415919104 | bytes 75497472 | tf_op jit(solution)/shard_map/pallas_call | solution.py:700
  65.2 2.4 %shard_map.167 = (bf16[16,8,32,128]{3,2,1,0:T(8,128)(2,1)}, bf16[16,8,32,128]{3,2,1,0:T(8,128)(2,1)}, bf16[16,768]{1,0:T(8,128)(2,1)}) custom-call(bf16[16,8,32,128]{3,2,1,0:T(8,128)(2,1)} %get-tuple-element.6.k_in, bf16[16,8,32,128]{3,2,1,0:T(8,128)(2,1)} %get-tuple-element.7.v_in, bf16[16,768]{1,0:T(8,128)(2,1)} %get-tuple-element.8.out_in), custom_call_target="tpu_custom_call" | custom-call | bytes 8388608 | tf_op jit(solution)/shard_map/pallas_call | solution.py:720

commit v4 on v3

--- a/solution.py
+++ b/solution.py
@@ -195,10 +195,10 @@
     wg_hbm, wu_hbm, wd_hbm, ids_ref, codes_ref,
     nk_hbm, nv_hbm, out_ref,
     ck, cv, rk, rv, sk, sv, nk, nv,
-    mask_ref, ws, cs, cr, ss, sr, attn_ref, po, pr, mixed_ref,
+    mask_ref, moved_mask, choose, mc, mr, ms, mt, ws, cs, cr, ss, sr, attn_ref, po, pr, mixed_ref,
     d1s, d1r, d2s, xr, acc_g, acc_u, hid, oacc, r1s, r1r, r2s, r2r, r3s, r3r, wt_ref,
     wbuf, wsem, csem, osem,
-    ms_send, ms_recv, a_send, a_recv, st_send, st_recv, p_send, p_recv,
+    ms_send, ms_recv, ma_send, ma_recv, mb_send, mb_recv, a_send, a_recv, st_send, st_recv, p_send, p_recv,
     e1_send, e1_recv, e2_send, e2_recv, e3_send, e3_recv,
     b1_send, b1_recv, b2_send, b2_recv, b3_send, b3_recv,
 ):
@@ -320,14 +320,6 @@
             move.start()
             moves.append(move)
 
-    lane = lax.broadcasted_iota(jnp.int32, (96, 16 * block_len), 1)
-    row = lax.broadcasted_iota(jnp.int32, (96, 16 * block_len), 0)
-    limit = jnp.zeros((96, 16 * block_len), jnp.int32)
-    for s in range(16):
-        limit = jnp.where(lane // block_len == s, lengths[s], limit)
-    inside = (d * block_len + lane % block_len <= limit) & (lane // block_len == row % 16)
-    mask_ref[...] = jnp.where(inside, 1.0, 0.0)
-
     expert_of = lax.broadcasted_iota(jnp.int32, (64, 16), 0) // 8
     slot_of = lax.broadcasted_iota(jnp.int32, (64, 16), 0) % 8
     codes = codes_ref[...].astype(F32)
@@ -356,6 +348,52 @@
             counts[i] = counts[i] + here
         places.append((off, jnp.minimum(at, 5)))
 
+    def insert(own, new, dst):
+        for s in range(16):
+            hit = p_iota == lengths[s] - d * block_len
+            fresh = jnp.broadcast_to(new[s].astype(F32)[:, None, :], (8, block_len, 128))
+            dst[s] = jnp.where(hit, fresh, own[s].astype(F32)).astype(BF)
+
+    def iota(shape, axis):
+        return lax.broadcasted_iota(jnp.int32, shape, axis)
+
+    columns = 16 * block_len
+    lane = iota((96, columns), 1)
+    limit = jnp.zeros((96, columns), jnp.int32)
+    for s, (off, _) in enumerate(places):
+        limit = jnp.where(lane // block_len == s, jnp.where(off == 0, lengths[s], -1), limit)
+    inside = (d * block_len + lane % block_len <= limit) & (
+        lane // block_len == iota((96, columns), 0) % 16
+    )
+    mask_ref[...] = jnp.where(inside, 1.0, 0.0)
+
+    holders = []
+    for a in range(6):
+        holder = jnp.int32(-1)
+        for s, (off, at) in enumerate(places):
+            holder = holder + ask(off != 0) * ask(at == a) * (s + 1)
+        holders.append(holder)
+
+    def held_by(shape):
+        place = iota(shape, 0) % 8
+        slot = jnp.full(shape, -1, jnp.int32)
+        for a, holder in enumerate(holders):
+            slot = jnp.where(place == a, holder, slot)
+        return slot
+
+    lane = iota((48, columns), 1)
+    limit = jnp.zeros((48, columns), jnp.int32)
+    for s in range(16):
+        limit = jnp.where(lane // block_len == s, lengths[s], limit)
+    inside = (d * block_len + lane % block_len <= limit) & (
+        lane // block_len == held_by((48, columns))
+    )
+    moved_mask[...] = jnp.where(inside, 1.0, 0.0)
+    chosen = (iota((48, 96), 0) // 8 == iota((48, 96), 1) // 16) & (
+        iota((48, 96), 1) % 16 == held_by((48, 96))
+    )
+    choose[...] = jnp.where(chosen, 1.0, 0.0).astype(BF)
+
     def build(own, got, new, dst):
         for s, (off, at) in enumerate(places):
             stays = jnp.full((8, block_len, 128), off, jnp.int32) == 0
@@ -364,80 +402,99 @@
             fresh = jnp.broadcast_to(new[s].astype(F32)[:, None, :], (8, block_len, 128))
             dst[s] = jnp.where(hit, fresh, kept).astype(BF)
 
+    def score(i, moved):
+        h = lax.rem(d + i, N)
+        rows = [
+            query[:, pl.ds(pl.multiple_of((h * 6 + j) * 128, 128), 128)] for j in range(6)
+        ]
+        q_h = jnp.concatenate(rows, axis=0)
+        if moved:
+            q_h = jnp.dot(choose[...], q_h, preferred_element_type=F32).astype(BF)
+        count = q_h.shape[0]
+        k_h = nk[:, pl.ds(h, 1)].reshape(columns, 128)
+        valid = (moved_mask if moved else mask_ref)[...] > 0.5
+        scores = lax.dot_general(q_h, k_h, (((1,), (1,)), ((), ())), preferred_element_type=F32)
+        scores = jnp.where(valid, scores / 128**0.5, F32(-1e30))
+        peak = jnp.max(scores, axis=1, keepdims=True)
+        weights = jnp.where(valid, jnp.exp(scores - peak), 0.0)
+        total = jnp.sum(weights, axis=1, keepdims=True)
+        ws[i, 0:count] = weights.astype(BF)
+        stat_lane = iota((count, 128), 1)
+        stat = jnp.where(stat_lane == 0, peak, jnp.where(stat_lane == 1, total, 0.0))
+        stat = jnp.concatenate([stat, jnp.zeros((128 - count, 128), F32)], axis=0)
+        (ms if moved else ss)[i] = jnp.transpose(stat)[0:8]
+
+    def score_all(moved):
+        def step(m, carry):
+            score(2 * m, moved)
+            score(2 * m + 1, moved)
+            return carry
+
+        lax.fori_loop(0, N // 2, step, 0)
+
+    def send_state(i, moved):
+        if moved:
+            return (
+                remote(mc.at[i], mr.at[i], ma_send.at[i], ma_recv.at[i], dev_peer(i)),
+                remote(ms.at[i], mt.at[i], mb_send.at[i], mb_recv.at[i], dev_peer(i)),
+            )
+        return (
+            remote(cs.at[i], cr.at[i], a_send.at[i], a_recv.at[i], dev_peer(i)),
+            remote(ss.at[i], sr.at[i], st_send.at[i], st_recv.at[i], dev_peer(i)),
+        )
+
+    def attend_all(moved):
+        count, out = (48, mc) if moved else (96, cs)
+        for i in (*range(1, N), 0):
+            v_h = nv[:, pl.ds(lax.rem(d + i, N), 1)].reshape(columns, 128)
+            out[i] = jnp.dot(ws[i, 0:count], v_h, preferred_element_type=F32).astype(BF)
+            if i:
+                for copy in send_state(i, moved):
+                    copy.start()
+
+    def merged(moved):
+        count, parts, stats = (48, mr, mt) if moved else (96, cr, sr)
+        for i in range(1, N):
+            for copy in send_state(i, moved):
+                copy.wait_recv()
+        peaks = jnp.concatenate([stats[i, 0:1] for i in range(N)], axis=0)
+        totals = jnp.concatenate([stats[i, 1:2] for i in range(N)], axis=0)
+        scale = jnp.exp(peaks - jnp.max(peaks, axis=0, keepdims=True))
+        norm = jnp.sum(scale * totals, axis=0, keepdims=True)
+        norm = jnp.where(norm > 0.0, norm, 1.0)
+        factor = jnp.concatenate([scale / norm, jnp.zeros((120, 128), F32)], axis=0)
+        factor = jnp.transpose(factor)
+        context = jnp.zeros((count, 128), F32)
+        for i in range(N):
+            context = context + parts[i].astype(F32) * factor[0:count, i : i + 1]
+        return context
+
+    insert(ck, new_key, nk)
+    insert(cv, new_value, nv)
+    score_all(False)
+    attend_all(False)
+    cr[0] = cs[0]
+    sr[0] = ss[0]
+
     for move in moves[: G - 1]:
         move.wait_recv()
     build(ck, rk, new_key, nk)
     put_k = pltpu.make_async_copy(nk, nk_hbm, osem.at[0])
     put_v = pltpu.make_async_copy(nv, nv_hbm, osem.at[1])
     put_k.start()
-
-    stat_lane = lax.broadcasted_iota(jnp.int32, (96, 128), 1)
-
-    def score(i):
-        h = lax.rem(d + i, N)
-        rows = [
-            query[:, pl.ds(pl.multiple_of((h * 6 + j) * 128, 128), 128)] for j in range(6)
-        ]
-        q_h = jnp.concatenate(rows, axis=0)
-        k_h = nk[:, pl.ds(h, 1)].reshape(16 * block_len, 128)
-        valid = mask_ref[...] > 0.5
-        scores = lax.dot_general(q_h, k_h, (((1,), (1,)), ((), ())), preferred_element_type=F32)
-        scores = jnp.where(valid, scores / 128**0.5, F32(-1e30))
-        peak = jnp.max(scores, axis=1, keepdims=True)
-        weights = jnp.where(valid, jnp.exp(scores - peak), 0.0)
-        total = jnp.sum(weights, axis=1, keepdims=True)
-        ws[i] = weights.astype(BF)
-        stat = jnp.where(stat_lane == 0, peak, jnp.where(stat_lane == 1, total, 0.0))
-        stat = jnp.concatenate([stat, jnp.zeros((32, 128), F32)], axis=0)
-        ss[i] = jnp.transpose(stat)[0:8]
-
-    def score_step(m, carry):
-        score(2 * m)
-        score(2 * m + 1)
-        return carry
-
-    lax.fori_loop(0, N // 2, score_step, 0)
-
-    def attend(i):
-        v_h = nv[:, pl.ds(lax.rem(d + i, N), 1)].reshape(16 * block_len, 128)
-        cs[i] = jnp.dot(ws[i], v_h, preferred_element_type=F32).astype(BF)
-
+    score_all(True)
     for move in moves[G - 1 :]:
         move.wait_recv()
     build(cv, rv, new_value, nv)
     put_v.start()
-
-    def send_state(i):
-        return (
-            remote(cs.at[i], cr.at[i], a_send.at[i], a_recv.at[i], dev_peer(i)),
-            remote(ss.at[i], sr.at[i], st_send.at[i], st_recv.at[i], dev_peer(i)),
-        )
-
-    def attend_step(i, carry):
-        attend(i)
-        for copy in send_state(i):
-            copy.start()
-        return carry
-
-    for i in range(1, N):
-        attend_step(i, 0)
-    attend(0)
-    cr[0] = cs[0]
-    sr[0] = ss[0]
-    for i in range(1, N):
-        for copy in send_state(i):
-            copy.wait_recv()
-
-    peaks = jnp.concatenate([sr[i, 0:1] for i in range(N)], axis=0)
-    totals = jnp.concatenate([sr[i, 1:2] for i in range(N)], axis=0)
-    scale = jnp.exp(peaks - jnp.max(peaks, axis=0, keepdims=True))
-    norm = jnp.sum(scale * totals, axis=0, keepdims=True)
-    norm = jnp.where(lax.broadcasted_iota(jnp.int32, (1, 128), 1) < 96, norm, 1.0)
-    factor = jnp.concatenate([scale / norm, jnp.zeros((120, 128), F32)], axis=0)
-    factor = jnp.transpose(factor)
-    context = jnp.zeros((96, 128), F32)
-    for i in range(N):
-        context = context + cr[i].astype(F32) * factor[0:96, i : i + 1]
+    attend_all(True)
+    mr[0] = mc[0]
+    mt[0] = ms[0]
+    context = merged(False)
+    arrived = merged(True).astype(BF)
+    context = context + lax.dot_general(
+        choose[...], arrived, (((0,), (0,)), ((), ())), preferred_element_type=F32
+    )
     for j in range(6):
         attn_ref[:, j * 128 : (j + 1) * 128] = context[j * 16 : (j + 1) * 16].astype(BF)
 
@@ -627,7 +684,7 @@
     for move in moves:
         move.wait_send()
     for i in range(1, N):
-        for copy in send_state(i):
+        for copy in (*send_state(i, False), *send_state(i, True)):
             copy.wait_send()
     core_partial().wait_send()
     for k in range(1, 4):
@@ -685,7 +742,9 @@
     scratch = [
         buf((16, *block)), buf((16, *block)), buf((6, *block)), buf((6, *block)),
         buf((6, *block)), buf((6, *block)), buf((16, *block)), buf((16, *block)),
-        buf((96, 16 * block[1]), F32), buf((8, 96, 16 * block[1])), buf((8, 96, 128)), buf((8, 96, 128)),
+        buf((96, 16 * block[1]), F32),
+        buf((48, 16 * block[1]), F32), buf((48, 96)), buf((8, 48, 128)), buf((8, 48, 128)),
+        buf((8, 8, 128), F32), buf((8, 8, 128), F32), buf((8, 96, 16 * block[1])), buf((8, 96, 128)), buf((8, 96, 128)),
         buf((8, 8, 128), F32), buf((8, 8, 128), F32), buf((16, feat)), buf((4, 16, 2 * feat)),
         buf((8, 16, feat)), buf((16, feat), F32),
         buf((4, 16, ext)), buf((4, 16, ext)), buf((2, 32, ext)), buf((8, 32, ext)),
@@ -693,7 +752,7 @@
         buf((4, 32, feat)), buf((4, 32, feat)), buf((4, 32, feat)), buf((4, 32, feat)),
         buf((4, 16, feat)), buf((4, 16, feat)), buf((2, 64, 16), F32),
         buf((SLOTS, feat, hidden)), dma((32,)), dma((2,)), dma((2,)),
-        dma((2, 4)), dma((2, 4)), dma((8,)), dma((8,)), dma((8,)), dma((8,)), dma((8,)), dma((8,)),
+        dma((2, 4)), dma((2, 4)), dma((8,)), dma((8,)), dma((8,)), dma((8,)), dma((8,)), dma((8,)), dma((8,)), dma((8,)), dma((8,)), dma((8,)),
         dma((4,)), dma((4,)), dma((4,)), dma((4,)), dma((4,)), dma((4,)),
         dma((4,)), dma((4,)), dma((4,)), dma((4,)), dma((4,)), dma((4,)),
     ]

time: 67.8 us -> 67.3 us (level)
  no operation moved by 1% of the time
where the time goes in v4:
time: 67.3 us; the launch traced here: 67.1 us
  Pallas kernels  66.5 us (99%)
    pallas_call x1, Pallas kernels, fused_layer(): pl.pallas_call(layer_kernel, out_shape=(jax.ShapeDtypeStruct(cache_k.shap...  64.1 us
    pallas_call x1, Pallas kernels, fused_layer(): pl.pallas_call(hand_over, out_shape=tuple((jax.ShapeDtypeStruct(r.shape,...  2.43 us

profile of v4, /device:TPU:0, one launch (start us, length us, event | category | flops | bytes accessed | tf_op | source)
XLA Modules:
  0.0 67.1 jit_solution(8457733417316159256)
XLA Ops:
  0.6 64.1 %shard_map.166 = (bf16[16,8,32,128]{3,2,1,0:T(8,128)(2,1)}, bf16[16,8,32,128]{3,2,1,0:T(8,128)(2,1)}, bf16[16,768]{1,0:T(8,128)(2,1)}) custom-call(bf16[16,8,32,128]{3,2,1,0:T(8,128)(2,1)} %ck_hbm.1, bf16[16,8,32,128]{3,2,1,0:T(8,128)(2,1)} %cv_hbm.1, s32[64]{0:T(128)} %source.1, s32[16]{0:T(128)} %lengths.1, bf16[16,6144]{1,0:T(8,128)(2,1)} %query.1, ...), custom_call_target="tpu_custom_call" | custom-call | flops 2415919104 | bytes 75497472 | tf_op jit(solution)/shard_map/pallas_call | solution.py:759
  64.7 2.4 %shard_map.167 = (bf16[16,8,32,128]{3,2,1,0:T(8,128)(2,1)}, bf16[16,8,32,128]{3,2,1,0:T(8,128)(2,1)}, bf16[16,768]{1,0:T(8,128)(2,1)}) custom-call(bf16[16,8,32,128]{3,2,1,0:T(8,128)(2,1)} %get-tuple-element.6.k_in, bf16[16,8,32,128]{3,2,1,0:T(8,128)(2,1)} %get-tuple-element.7.v_in, bf16[16,768]{1,0:T(8,128)(2,1)} %get-tuple-element.8.out_in), custom_call_target="tpu_custom_call" | custom-call | bytes 8388608 | tf_op jit(solution)/shard_map/pallas_call | solution.py:779
